TPU v7x, 32 devices: a whole 2x2x4 slice. The times are simulated.
32 devices in a mesh: pipe: 4 (over y, x), dp: 8 (over z, core).
Axes of the slice: x: 2, y: 2, z: 4, core: 2. Of those that a mesh axis runs over, the one named last changes fastest.
Arguments:
- source: bfloat16 [16, 1024, 512], P('dp', 'pipe'), may hold values from -6 to 6
- target: bfloat16 [16, 1024, 512], P('dp', 'pipe'), may hold values from -6 to 6
- source_length: int32 [16], P('dp'), may hold values from 128 to 1024, as said below
- target_length: int32 [16], P('dp'), may hold values from 128 to 1024, as said below
- memory_cotangent: bfloat16 [16, 1024, 512], P('dp', 'pipe'), may hold values from -6 to 6
- output_cotangent: bfloat16 [16, 1024, 512], P('dp', 'pipe'), may hold values from -6 to 6
- source_query: bfloat16 [512, 512], replicated, may hold values from -0.25 to 0.25
- source_keyvalue: bfloat16 [512, 1024], replicated, may hold values from -0.25 to 0.25
- source_output: bfloat16 [512, 512], replicated, may hold values from -3 to 3
- source_gain: float32 [512], replicated, may hold values from 0.25 to 1.75
- source_offset: float32 [512], replicated, may hold values from -3 to 3
- source_expand: bfloat16 [512, 2048], replicated, may hold values from -0.25 to 0.25
- source_bias: float32 [2048], replicated, may hold values from -3 to 3
- source_contract: bfloat16 [2048, 512], replicated, may hold values from -0.125 to 0.125
- source_shift: float32 [512], replicated, may hold values from -3 to 3
- source_scale: float32 [512], replicated, may hold values from 0.25 to 1.75
- source_center: float32 [512], replicated, may hold values from -3 to 3
- target_query: bfloat16 [512, 512], replicated, may hold values from -0.25 to 0.25
- target_keyvalue: bfloat16 [512, 1024], replicated, may hold values from -0.25 to 0.25
- target_output: bfloat16 [512, 512], replicated, may hold values from -3 to 3
- target_gain: float32 [512], replicated, may hold values from 0.25 to 1.75
- target_offset: float32 [512], replicated, may hold values from -3 to 3
- cross_query: bfloat16 [512, 512], replicated, may hold values from -0.25 to 0.25
- cross_keyvalue: bfloat16 [512, 1024], replicated, may hold values from -0.25 to 0.25
- cross_output: bfloat16 [512, 512], replicated, may hold values from -3 to 3
- cross_gain: float32 [512], replicated, may hold values from 0.25 to 1.75
- cross_offset: float32 [512], replicated, may hold values from -3 to 3
- target_expand: bfloat16 [512, 2048], replicated, may hold values from -0.25 to 0.25
- target_bias: float32 [2048], replicated, may hold values from -3 to 3
- target_contract: bfloat16 [2048, 512], replicated, may hold values from -0.125 to 0.125
- target_shift: float32 [512], replicated, may hold values from -3 to 3
- target_scale: float32 [512], replicated, may hold values from 0.25 to 1.75
- target_center: float32 [512], replicated, may hold values from -3 to 3
Outputs:
- encoder_output: bfloat16 [16, 1024, 512], P('dp', 'pipe')
- decoder_output: bfloat16 [16, 1024, 512], P('dp', 'pipe')
- source_gradient: float32 [16, 1024, 512], P('dp', 'pipe')
- target_gradient: float32 [16, 1024, 512], P('dp', 'pipe')
- source_query_gradient: float32 [512, 512], P('dp')
- source_keyvalue_gradient: float32 [512, 1024], P('dp')
- source_output_gradient: float32 [512, 512], P('dp')
- source_gain_gradient: float32 [512], P('dp')
- source_offset_gradient: float32 [512], P('dp')
- source_expand_gradient: float32 [512, 2048], P('dp')
- source_bias_gradient: float32 [2048], P('dp')
- source_contract_gradient: float32 [2048, 512], P('dp')
- source_shift_gradient: float32 [512], P('dp')
- source_scale_gradient: float32 [512], P('dp')
- source_center_gradient: float32 [512], P('dp')
- target_query_gradient: float32 [512, 512], P('dp')
- target_keyvalue_gradient: float32 [512, 1024], P('dp')
- target_output_gradient: float32 [512, 512], P('dp')
- target_gain_gradient: float32 [512], P('dp')
- target_offset_gradient: float32 [512], P('dp')
- cross_query_gradient: float32 [512, 512], P('dp')
- cross_keyvalue_gradient: float32 [512, 1024], P('dp')
- cross_output_gradient: float32 [512, 512], P('dp')
- cross_gain_gradient: float32 [512], P('dp')
- cross_offset_gradient: float32 [512], P('dp')
- target_expand_gradient: float32 [512, 2048], P('dp')
- target_bias_gradient: float32 [2048], P('dp')
- target_contract_gradient: float32 [2048, 512], P('dp')
- target_shift_gradient: float32 [512], P('dp')
- target_scale_gradient: float32 [512], P('dp')
- target_center_gradient: float32 [512], P('dp')
Inputs may be any that keep to these rules, and one draw needn't show every extreme that they name: `source_length`: the number of real tokens of each source sequence; some sequence has all 1024. `target_length`: the number of real tokens of each target sequence; some sequence has all 1024.
All inputs are finite; a program needn't handle non-finite values.
Results may differ from a plain program's by a relative error of at most 0.024.
Values may be sent and summed in bfloat16 or wider, within the bound.
No kernel may reach another device: no remote copies, remote signals or barrier semaphores. Data moves between devices by JAX's collectives and lax.ppermute only.
A program may use at most 320 MiB of HBM per device.

v0:
```python
import functools

import jax
import jax.numpy as jnp
from jax import lax
from jax.experimental import pallas as pl
from jax.experimental.pallas import tpu as pltpu
from jax.sharding import PartitionSpec as P

HEAD_DIM = 64
PAIR = 2 * HEAD_DIM
LOG2E = 1.4426950408889634
LN2 = 0.6931471805599453
HIDDEN = -1e30
BF = jnp.bfloat16
F32 = jnp.float32
VMEM_BYTES = 56 * 2**20
SMALL_BYTES = 16 * 2**20


def product(left, right, sides):
    return lax.dot_general(left, right, (sides, ((), ())), preferred_element_type=F32)


def nn(left, right):
    return product(left, right, ((1,), (0,)))


def nt(left, right):
    return product(left, right, ((1,), (1,)))


def tn(left, right):
    return product(left, right, ((0,), (0,)))


def norm_forward(value):
    center = value - jnp.mean(value, -1, keepdims=True)
    inverse = lax.rsqrt(jnp.mean(center * center, -1, keepdims=True) + 1e-05)
    return center * inverse, inverse


def norm_backward(gradient, normed, inverse, gain):
    scaled = gradient * gain
    back = inverse * (
        scaled
        - jnp.mean(scaled, -1, keepdims=True)
        - normed * jnp.mean(scaled * normed, -1, keepdims=True)
    )
    return (
        back,
        jnp.sum(gradient * normed, 0, keepdims=True),
        jnp.sum(gradient, 0, keepdims=True),
    )


def fill_bias(place_ref, count, causal, bias_ref):
    keys, width = bias_ref.shape
    rows = keys // 4
    for block in range(4):
        first = block * rows if causal else place_ref[block]
        at = first + lax.broadcasted_iota(jnp.int32, (rows, width), 0)
        allowed = at < count
        if causal:
            lane = lax.broadcasted_iota(jnp.int32, (rows, width), 1)
            asked = jnp.where(lane < rows, place_ref[0] + lane, place_ref[1] + lane - rows)
            allowed = allowed & (at <= asked)
        bias_ref[block * rows : (block + 1) * rows, :] = jnp.where(allowed, 0.0, HIDDEN)


def by_core(place_ref, rows, keys, run):
    block = rows // 2
    for core in range(2):
        seen = (core + 1, keys // block - core)

        @pl.when(place_ref[6] == core)
        def _(seen=seen):
            run(tuple((at * block, (at + 1) * block, count * block) for at, count in enumerate(seen)))


def bias_of(bias_ref, first, last, keys):
    width = bias_ref.shape[1]
    if width > 128:
        return bias_ref[:keys, first:last]
    return jnp.concatenate([bias_ref[:keys, :]] * ((last - first) // width), 1)


def head_lanes(half):
    lane = lax.broadcasted_iota(jnp.int32, (1, PAIR), 1)
    return (lane >= HEAD_DIM * half) & (lane < HEAD_DIM * (half + 1))


def project(own, other_ref, wq, wkv, q_ref, k_ref, v_ref, own_keys=None, starts=None):
    rows, width = own.shape
    q_ref[...] = (nn(own, wq[...]) * (HEAD_DIM**-0.5 * LOG2E)).astype(BF)
    keys = own if own_keys is None else own_keys
    for at in (0, rows):
        for ref, part in ((k_ref, wkv[:, :width]), (v_ref, wkv[:, width:])):
            value = nn(keys, part).astype(BF)
            if starts is None:
                ref[at : at + rows, :] = value
                continue
            block = rows // 2
            for half in range(2):
                first = pl.multiple_of(starts[2 * at // rows + half], block)
                ref[pl.ds(first, block), :] = value[half * block : (half + 1) * block]
        keys = other_ref[...]


def attend(spans, step, q_ref, k_ref, v_ref, bias_ref, ot_ref, lse_ref):
    def one_head(index, half):
        cols = pl.ds(pl.multiple_of(index // 2 * PAIR, PAIR), PAIR)
        at = pl.multiple_of(index * HEAD_DIM, HEAD_DIM)
        values = v_ref[:, cols].T
        if isinstance(half, int):
            values = values[HEAD_DIM * half : HEAD_DIM * (half + 1)]
        else:
            values = jnp.where(half == 0, values[:HEAD_DIM], values[HEAD_DIM:])
        for first, last, seen in spans:
            queries, keys = q_ref[first:last, cols], k_ref[:seen, cols]
            masked = jnp.where(head_lanes(half), queries, jnp.zeros_like(queries))
            scores = nt(keys, masked) + bias_of(bias_ref, first, last, seen)
            top = jnp.max(scores, 0, keepdims=True)
            expon = jnp.exp2(scores - top)
            total = jnp.sum(expon, 0, keepdims=True)
            mixed = nn(values[:, :seen], expon.astype(BF))
            ot_ref[pl.ds(at, HEAD_DIM), first:last] = mixed / total
            lse_ref[pl.ds(index, 1), first:last] = top + jnp.log2(total)

    def heads(index, carry):
        for half in range(step):
            one_head(step * index + half, half if step == 2 else index % 2)
        return carry

    lax.fori_loop(0, q_ref.shape[1] // HEAD_DIM // step, heads, 0)


def attend_back(
    spans, q_ref, k_ref, v_ref, do_ref, bias_ref, lse_ref, delta_ref, dqt_ref, dk_ref, dv_ref
):
    def pair(index, carry):
        cols = pl.ds(pl.multiple_of(index * PAIR, PAIR), PAIR)
        turned = k_ref[:, cols].T
        done = 0
        for first, last, seen in spans:
            keys, values = k_ref[:seen, cols], v_ref[:seen, cols]
            queries, grads = q_ref[first:last, cols], do_ref[first:last, cols]
            dkeys = dvalues = None
            for half in range(2):
                mine = head_lanes(half)
                masked = jnp.where(mine, queries, jnp.zeros_like(queries))
                masked_grads = jnp.where(mine, grads, jnp.zeros_like(grads))
                head = pl.ds(2 * index + half, 1)
                scores = nt(keys, masked) + bias_of(bias_ref, first, last, seen)
                probs = jnp.exp2(scores - lse_ref[head, first:last])
                dprobs = nt(values, masked_grads)
                dscores = (probs * (dprobs - delta_ref[head, first:last])).astype(BF)
                part = nn(probs.astype(BF), masked_grads)
                dvalues = part if half == 0 else dvalues + part
                part = nn(dscores, masked)
                dkeys = part if half == 0 else dkeys + part
                dquery = nn(turned[HEAD_DIM * half : HEAD_DIM * (half + 1), :seen], dscores)
                at = pl.multiple_of(index * PAIR + HEAD_DIM * half, HEAD_DIM)
                dqt_ref[pl.ds(at, HEAD_DIM), first:last] = (dquery * HEAD_DIM**-0.5).astype(BF)
            dkeys = dkeys * LN2
            if done:
                dkeys = jnp.concatenate([dkeys[:done] + dk_ref[:done, cols].astype(F32), dkeys[done:]], 0)
                dvalues = jnp.concatenate([dvalues[:done] + dv_ref[:done, cols].astype(F32), dvalues[done:]], 0)
            dk_ref[:seen, cols] = dkeys.astype(BF)
            dv_ref[:seen, cols] = dvalues.astype(BF)
            done = seen
        if done < k_ref.shape[0]:
            rest = jnp.zeros((k_ref.shape[0] - done, PAIR), BF)
            dk_ref[done:, cols] = rest
            dv_ref[done:, cols] = rest
        return carry

    lax.fori_loop(0, q_ref.shape[1] // PAIR, pair, 0)


class Spread:
    def __init__(self, core, keep_ref, send_ref):
        self.first = core == 0
        self.keep_ref, self.send_ref = keep_ref, send_ref
        self.quarters, self.planes, self.rows = keep_ref.shape[:3]

    def put(self, quarter, plane, at, even, odd):
        even, odd = even.astype(BF), odd.astype(BF)
        rows = slice(at, at + even.shape[0])
        self.keep_ref[quarter, plane, rows, :] = jnp.where(self.first, even, odd)
        self.send_ref[quarter, plane, rows, :] = jnp.where(self.first, odd, even)

    def square(self, value, at):
        chunk = value.shape[0] // (2 * self.planes)
        piece = chunk // self.quarters
        for plane in range(self.planes):
            for quarter in range(self.quarters):
                even = 2 * plane * chunk + quarter * piece
                odd = even + chunk
                self.put(quarter, plane, at, value[even : even + piece], value[odd : odd + piece])

    def columns(self, value, quarter, at):
        chunk = value.shape[0] // (2 * self.planes)
        for plane in range(self.planes):
            even = 2 * plane * chunk
            odd = even + chunk
            self.put(quarter, plane, at, value[even : even + chunk], value[odd : odd + chunk])

    def two_chunks(self, value, plane, at):
        chunk = value.shape[0] // 2
        piece = chunk // self.quarters
        for quarter in range(self.quarters):
            even = quarter * piece
            odd = even + chunk
            self.put(quarter, plane, at, value[even : even + piece], value[odd : odd + piece])

    def same(self, quarter, at, value):
        for plane in range(self.planes):
            self.put(quarter, plane, at, value, value)


class Chunks(Spread):
    def __init__(self, ref):
        self.ref = ref
        self.quarters, self.planes, self.rows = ref.shape[1], ref.shape[0] // 2, ref.shape[2]

    def put(self, quarter, plane, at, even, odd):
        rows = slice(at, at + even.shape[0])
        self.ref[2 * plane, quarter, rows, :] = even.astype(BF)
        self.ref[2 * plane + 1, quarter, rows, :] = odd.astype(BF)


class Whole:
    def __init__(self, refs):
        self.refs = refs


def spread_of(io, refs):
    if isinstance(refs, list) and len(refs) == 2:
        return Spread(io.place[6], *refs)
    if isinstance(refs, list):
        return Whole(refs)
    return Chunks(refs)


def spread_attention(spread, own, keys_own, keys_other, dar, ot_ref, dqt_ref, dk, dv):
    rows, width = dar.shape
    dq = dqt_ref[...].T
    own_t = own[...].T
    keys_t = own_t if keys_own is own else keys_own[...].T
    other_t = keys_other[...].T
    dwo = nn(ot_ref[...].astype(BF), dar)
    dwq = nn(own_t, dq)
    dwk = nn(keys_t, dk[0]) + nn(other_t, dk[1])
    dwv = nn(keys_t, dv[0]) + nn(other_t, dv[1])
    if isinstance(spread, Whole):
        wq_ref, wkv_ref, wo_ref = spread.refs
        wq_ref[...] = dwq.astype(BF)
        wkv_ref[:, :width] = dwk.astype(BF)
        wkv_ref[:, width:] = dwv.astype(BF)
        wo_ref[...] = dwo.astype(BF)
        return
    piece = spread.rows // 4
    for place, value in enumerate((dwq, dwk, dwv, dwo)):
        spread.square(value, place * piece)


BLOCK = 512
TANH_SCALE = 0.7978845608028654
TANH_CUBE = 0.044715


def expand(hidden, w1, b1, active_ref, slope_ref):
    for at in range(0, w1.shape[1], BLOCK):
        cols = slice(at, at + BLOCK)
        before = nn(hidden, w1[:, cols]) + b1[:, cols]
        square = before * before
        inner = before * (TANH_SCALE + (TANH_SCALE * TANH_CUBE) * square)
        curve = jnp.tanh(inner)
        half = 0.5 * (1.0 + curve)
        active_ref[:, cols] = (before * half).astype(BF)
        steep = TANH_SCALE + (3 * TANH_SCALE * TANH_CUBE) * square
        slope_ref[:, cols] = (half + (0.5 * before) * (1.0 - curve * curve) * steep).astype(BF)


def contract(hidden, residual, active_ref, w2, b2):
    total = hidden.astype(F32) + nn(active_ref[...], w2[...]) + b2[...] + residual.astype(F32)
    return norm_forward(total)


def ffn_backward(io, spread, back, hidden, parts, bias_grad_ref):
    low = back.astype(BF)
    hidden_t = hidden.T
    dhidden = None
    for number in range(bias_grad_ref.shape[0]):
        w1, w2, active, slope = parts(number)
        dactive = nt(low, w2).astype(BF)
        dbefore = (dactive.astype(F32) * slope.astype(F32)).astype(BF)
        bias_grad_ref[number : number + 1, :] = jnp.sum(dbefore.astype(F32), 0, keepdims=True)
        dcontract = tn(active, low)
        dexpand = nn(hidden_t, dbefore)
        if isinstance(spread, Whole):
            block = slice(number * BLOCK, (number + 1) * BLOCK)
            spread.refs[0][:, block] = dexpand.astype(BF)
            spread.refs[1][block, :] = dcontract.astype(BF)
        else:
            chunk = dexpand.shape[0] // (2 * spread.planes)
            spread.columns(dexpand, number, 0)
            spread.two_chunks(dcontract, number, chunk)
            io.send_part(spread.ref, 2 * number, (slice(None), number, slice(0, chunk)))
            pair = slice(2 * number, 2 * number + 2)
            io.send_part(spread.ref, 2 * number + 1, (pair, slice(None), slice(chunk, 2 * chunk)))
        part = nt(dbefore, w1)
        dhidden = part if dhidden is None else dhidden + part
    return dhidden, jnp.sum(low.astype(F32), 0, keepdims=True)


PARTS = 12


class Buffers:
    def __init__(self, place, ins, outs, small):
        self.place, self.ins, self.outs, self.small = place, ins, outs, small
        self.waiting, self.going = {}, []
        self.queue, late = [], []
        for name, entry in ins.items():
            if entry is None:
                self.ahead()
                continue
            buffer, sources, sems = entry
            copies = [
                pltpu.make_async_copy(source, buffer.at[where], sems.at[number])
                for number, (source, where) in enumerate(sources)
            ]
            self.waiting[name] = copies
            if len(copies) > 2:
                late.append(copies)
            else:
                self.queue += copies
        for copies in zip(*late, strict=True):
            self.queue += copies
        if None not in ins.values():
            self.ahead()
        self.sent = set()

    def __getattr__(self, name):
        if name in self.small:
            return self.small[name]
        if name in self.outs:
            buffers = self.outs[name]
            return [buffer for buffer, _, _ in buffers] if isinstance(buffers, list) else buffers[0]
        for copy in self.waiting[name]:
            self.wait(copy)
        self.waiting[name] = []
        return self.ins[name][0]

    def block(self, name, number):
        self.wait(self.waiting[name][number])
        if number + 1 == len(self.waiting[name]):
            self.waiting[name] = []
        return self.ins[name][0]

    def ahead(self):
        for copy in self.queue:
            copy.start()
        self.queue = []

    def wait(self, copy):
        if any(copy is other for other in self.queue):
            self.ahead()
        copy.wait()

    def results(self):
        for entry in self.outs.values():
            yield from entry if isinstance(entry, list) else [entry]

    def start(self, copy):
        copy.start()
        self.going.append(copy)

    def send(self, *refs):
        for buffer, targets, sems in self.results():
            if any(buffer is ref for ref in refs):
                self.sent.add(id(buffer))
                for number, (target, where) in enumerate(targets):
                    self.start(pltpu.make_async_copy(buffer.at[where], target, sems.at[number]))

    def send_part(self, ref, number, where):
        for buffer, targets, sems in self.results():
            if buffer is ref:
                self.sent.add(id(buffer))
                self.start(
                    pltpu.make_async_copy(buffer.at[where], targets[0][0].at[where], sems.at[number])
                )

    def finish(self):
        self.send(*[entry[0] for entry in self.results() if id(entry[0]) not in self.sent])
        for copies in self.waiting.values():
            for copy in copies:
                self.wait(copy)
        for copy in self.going:
            copy.wait()


class Part:
    def __init__(self, io, prefix):
        self.io, self.prefix = io, prefix
        self.place, self.send, self.ahead = io.place, io.send, io.ahead

    def __getattr__(self, name):
        return getattr(self.io, self.prefix + name)


class Ends(list):
    pass


class Blocks:
    def __init__(self, array, axis):
        self.array, self.axis = array, axis


def run(kernel, name, flops, place, ins, small, outs, scratch=(), vmem_bytes=VMEM_BYTES):
    arrays, buffers, sem_counts, shapes = [], [], [], []
    in_plan, out_plan = {}, {}

    def buffer(dims, dtype, sems):
        buffers.append(pltpu.VMEM(tuple(dims), dtype))
        sem_counts.append(sems)
        return len(buffers) - 1

    for key, value in ins.items():
        if value is None:
            in_plan[key] = None
            continue
        plan = []
        if isinstance(value, Blocks):
            array, axis = value.array, value.axis
            for at in range(0, array.shape[axis], BLOCK):
                where = (slice(None),) * axis + (slice(at, at + BLOCK),)
                plan.append((len(arrays), where, where))
            arrays.append(array)
            dims, dtype = array.shape, array.dtype
        else:
            rows = 0
            for part in value if isinstance(value, Ends) else [value]:
                array, index = part if isinstance(part, tuple) else (part, None)
                dims = array.shape if index is None else array.shape[1:]
                where = len(plan) if isinstance(value, Ends) else ()
                plan.append((len(arrays), () if index is None else (index,), where))
                rows += dims[0]
                arrays.append(array)
            dims, dtype = (rows, *dims[1:]), array.dtype
        in_plan[key] = (buffer(dims, dtype, len(plan)), plan)

    def plan_out(value):
        if isinstance(value, Ends):
            plan = [(len(shapes) + number, number) for number in range(len(value))]
            shapes.extend(value)
            rows = sum(part.shape[0] for part in value)
            return buffer((rows, *value[0].shape[1:]), value[0].dtype, len(plan)), plan
        shapes.append(value)
        return buffer(value.shape, value.dtype, PARTS), [(len(shapes) - 1, ())]

    for key, value in outs.items():
        whole = isinstance(value, list) and not isinstance(value, Ends)
        out_plan[key] = [plan_out(part) for part in value] if whole else plan_out(value)

    def body(place_ref, *refs):
        cuts = (len(small), len(arrays), len(shapes), len(buffers), len(sem_counts))
        groups, at = [], 0
        for count in cuts:
            groups.append(refs[at : at + count])
            at += count
        small_refs, in_refs, out_refs, buffer_refs, sems = groups

        def part_of(ref, where):
            return ref.at[where] if where else ref

        def settled(where, rows):
            if not isinstance(where, int):
                return where
            return (pl.ds(pl.multiple_of((place_ref[9] ^ where) * rows, rows), rows),)

        def out_entry(plan):
            number, targets = plan
            return (
                buffer_refs[number],
                [(out_refs[which], settled(where, out_refs[which].shape[0])) for which, where in targets],
                sems[number],
            )

        def in_entry(number, plan):
            parts = []
            for which, where, to in plan:
                source = part_of(in_refs[which], where)
                parts.append((source, settled(to, source.shape[0])))
            return buffer_refs[number], parts, sems[number]

        in_map = {key: plan and in_entry(*plan) for key, plan in in_plan.items()}
        out_map = {
            key: [out_entry(part) for part in plan] if isinstance(plan, list) else out_entry(plan)
            for key, plan in out_plan.items()
        }
        io = Buffers(place_ref, in_map, out_map, dict(zip(small, small_refs, strict=True)))
        kernel(io, *refs[at:])
        io.finish()

    vmem, anywhere = pl.BlockSpec(memory_space=pltpu.VMEM), pl.BlockSpec(memory_space=pl.ANY)
    moved = sum(a.size * a.dtype.itemsize for a in (*arrays, *shapes))
    results = pl.pallas_call(
        body,
        out_shape=shapes,
        in_specs=[pl.BlockSpec(memory_space=pltpu.SMEM)] + [vmem] * len(small) + [anywhere] * len(arrays),
        out_specs=[anywhere] * len(shapes),
        scratch_shapes=[*buffers, *[pltpu.SemaphoreType.DMA((count,)) for count in sem_counts], *scratch],
        name=name,
        cost_estimate=pl.CostEstimate(flops=flops, bytes_accessed=moved, transcendentals=0),
        compiler_params=pltpu.CompilerParams(vmem_limit_bytes=vmem_bytes),
    )(place, *small.values(), *arrays)

    def named(plan):
        if isinstance(plan, list):
            return [named(part) for part in plan]
        got = [results[which] for which, _ in plan[1]]
        return got if len(got) > 1 else got[0]

    return Results({key: named(plan) for key, plan in out_plan.items()})


class Results(dict):
    def __getattr__(self, name):
        return self[name]


def put_norm(io, normed, inverse, normed_ref, inverse_ref):
    normed_ref[...] = normed
    inverse_ref[...] = jnp.broadcast_to(inverse, inverse_ref.shape)
    io.send(normed_ref, inverse_ref)


def self_attention(io, count_at, causal, bias_ref):
    fill_bias(io.place, io.place[count_at], causal, bias_ref)
    rows = io.own[...]
    starts = [io.place[block] for block in range(4)] if causal else None
    project(rows, io.other, io.wq, io.wkv, io.q, io.k, io.v, starts=starts)
    io.send(io.q, io.k, io.v)
    io.ahead()
    q, k, v, ot, lse = io.q, io.k, io.v, io.ot, io.lse
    whole = ((0, q.shape[0], k.shape[0]),)
    attend(whole, 2, q, k, v, bias_ref, ot, lse)
    io.send(ot, lse)
    return tn(ot[...].astype(BF), io.wo[...]), rows


def run_spans(io, causal, run):
    rows, keys = io.q.shape[0], io.k.shape[0]
    if causal:
        by_core(io.place, rows, keys, run)
    else:
        run(((0, rows, keys),))


def encoder_forward_kernel(io, bias_ref):
    attn, rows = self_attention(io, 4, False, bias_ref)
    normed, inverse = norm_forward(rows.astype(F32) + attn)
    put_norm(io, normed, inverse, io.n0, io.i0)
    hidden = (normed * io.gain[...] + io.offset[...]).astype(BF)
    io.hidden[...] = hidden
    io.send(io.hidden)
    expand(hidden, io.w1, io.b1, io.active, io.slope)
    io.send(io.active, io.slope)
    normed, inverse = contract(hidden, rows, io.active, io.w2, io.b2)
    io.memory[...] = (normed * io.scale[...] + io.center[...]).astype(BF)
    io.send(io.memory)
    put_norm(io, normed, inverse, io.n1, io.i1)


def decoder_forward_kernel(io, causal_ref, bias_ref, active_ref, slope_ref):
    attn, rows = self_attention(Part(io, "s"), 5, True, causal_ref)
    normed, inverse = norm_forward(rows.astype(F32) + attn)
    put_norm(io, normed, inverse, io.n, io.i)
    spread = spread_of(io, io.grads)
    fill_bias(io.place, io.place[4], False, bias_ref)
    first = io.n[...] * io.gain[...] + io.offset[...]
    first_low = first.astype(BF)
    io.first[...] = first_low
    io.send(io.first)
    memory = io.mem_own[...]
    project(first_low, io.mem_other, io.wq, io.wkv, io.q, io.k, io.v, memory)
    io.send(io.q, io.k, io.v)
    io.ahead()
    q, k, v, ot, lse = io.q, io.k, io.v, io.ot, io.lse
    whole = ((0, q.shape[0], k.shape[0]),)
    attend(whole, 2, q, k, v, bias_ref, ot, lse)
    io.send(io.ot, io.lse)
    n2, i2 = norm_forward(first + tn(io.ot[...].astype(BF), io.wo[...]))
    second = (n2 * io.cross_gain[...] + io.cross_offset[...]).astype(BF)
    expand(second, io.w1, io.b1, active_ref, slope_ref)
    n3, i3 = contract(second, io.sown[...], active_ref, io.w2, io.b2)
    output = (n3 * io.scale[...] + io.center[...]).astype(BF)
    block = output.shape[0] // 2
    for half in range(2):
        rows = slice(half * block, (half + 1) * block)
        io.result[2 * half] = memory[rows]
        io.result[2 * half + 1] = output[rows]
    io.send(io.result)
    back, dscale, dcenter = norm_backward(io.cotangent[...].astype(F32), n3, i3, io.scale[...])
    io.dr[...] = back
    io.send(io.dr)
    w1, w2 = io.w1, io.w2

    def parts(number):
        cut = slice(number * BLOCK, (number + 1) * BLOCK)
        return w1[:, cut], w2[cut, :], active_ref[:, cut], slope_ref[:, cut]

    vecs = io.vecs
    dhidden, dshift = ffn_backward(io, spread, back, second, parts, vecs.at[0:4])
    dsecond = (back + dhidden).astype(BF).astype(F32)
    dv2, dgain, doffset = norm_backward(dsecond, n2, i2, io.cross_gain[...])
    io.dv[...] = dv2
    io.send(io.dv)
    put_rows(vecs, 4, (dshift, dscale, dcenter, dgain, doffset))


def put_rows(ref, at, values):
    for row, value in enumerate(values):
        ref[at + row : at + row + 1, :] = value
    at += len(values)
    ref[at:, :] = jnp.zeros((ref.shape[0] - at, ref.shape[1]), F32)


def cross_backward_kernel(io, bias_ref, *scratch):
    fill_bias(io.place, io.place[4], False, bias_ref)
    dv2 = io.dv[...]
    du, dc_own, dc_other = attention_backward(
        io, False, bias_ref, scratch, dv2.astype(BF), "first", "mem_own", "mem_other"
    )
    io.dmem_other[...] = dc_other.astype(BF)
    io.dmem_own[...] = dc_own.astype(BF)
    io.send(io.dmem_other, io.dmem_own)
    dv1, dgain, doffset = norm_backward(dv2 + du, io.n[...], io.i[:, :1], io.gain[...])
    io.dv1[...] = dv1
    io.send(io.dv1)
    put_rows(io.vecs, 0, (dgain, doffset))


def self_backward(io, count_at, causal, bias_ref, scratch):
    fill_bias(io.place, io.place[count_at], causal, bias_ref)
    dv = io.dv[...]
    du, dc_own, dc_other = attention_backward(
        io, causal, bias_ref, scratch, dv.astype(BF), "own", "own", "other"
    )
    io.dc_other[...] = dc_other.astype(BF)
    io.send(io.dc_other)
    io.du[...] = (dv + io.extra[...] + du + dc_own).astype(BF)
    io.send(io.du)


def source_backward_kernel(io, bias_ref, *scratch):
    self_backward(io, 4, False, bias_ref, scratch)


def target_backward_kernel(io, bias_ref, *scratch):
    self_backward(io, 5, True, bias_ref, scratch)


def attention_backward(io, causal, bias_ref, scratch, dar, own, keys_own, keys_other):
    spread = spread_of(io, io.grads)
    do_ref, delta_ref, dqt_ref, dk_ref, dv_ref = scratch
    rows, width = dar.shape
    wo, ot = io.wo, io.ot
    do_ref[...] = nt(dar, wo[...]).astype(BF)
    turned = nt(wo[...], dar).astype(BF).astype(F32) * ot[...]
    delta_ref[...] = jnp.sum(turned.reshape(width // HEAD_DIM, HEAD_DIM, rows), 1)
    queries, keys, values, lse = io.q, io.k, io.v, io.lse
    io.ahead()
    run_spans(
        io,
        causal,
        lambda spans: attend_back(
            spans, queries, keys, values, do_ref, bias_ref, lse, delta_ref, dqt_ref, dk_ref, dv_ref
        ),
    )
    if causal:
        starts = [io.place[block] for block in range(4)]
        dk, dv = [
            [
                jnp.concatenate([ref[pl.ds(pl.multiple_of(first, rows // 2), rows // 2), :] for first in firsts], 0)
                for firsts in (starts[:2], starts[2:])
            ]
            for ref in (dk_ref, dv_ref)
        ]
    else:
        dk, dv = [[ref[:rows, :], ref[rows:, :]] for ref in (dk_ref, dv_ref)]
    own_ref = getattr(io, own)
    keys_ref = own_ref if keys_own == own else getattr(io, keys_own)
    spread_attention(spread, own_ref, keys_ref, getattr(io, keys_other), dar, ot, dqt_ref, dk, dv)
    io.send(*io.grads)
    dq = dqt_ref[...].T
    wkv = io.wkv
    dc = [
        nt(dk[at], wkv[:, :width]) + nt(dv[at], wkv[:, width:])
        for at in (1, 0)
    ]
    return nt(dq, io.wq[...]), dc[1], dc[0]


def encoder_ffn_backward(io):
    spread = spread_of(io, io.grads)
    dmemory = (io.dmem_own[...].astype(F32) + io.dmem_came[...].astype(F32)).astype(BF).astype(F32)
    total = io.cotangent[...].astype(F32) + dmemory
    back, dscale, dcenter = norm_backward(total, io.n1[...], io.i1[:, :1], io.scale[...])
    io.dr[...] = back
    io.send(io.dr)

    def parts(number):
        cut = slice(number * BLOCK, (number + 1) * BLOCK)
        return (
            io.block("w1", number)[:, cut],
            io.block("w2", number)[cut, :],
            io.block("active", number)[:, cut],
            io.block("slope", number)[:, cut],
        )

    vecs = io.vecs
    dhidden, dshift = ffn_backward(io, spread, back, io.hidden[...], parts, vecs.at[0:4])
    dlow = (back + dhidden).astype(BF).astype(F32)
    dv0, dgain, doffset = norm_backward(dlow, io.n0[...], io.i0[:, :1], io.gain[...])
    io.dv[...] = dv0
    io.send(io.dv)
    top, cross = io.top_vecs, io.cross_vecs
    rest = [top[row : row + 1, :] for row in range(9)] + [cross[row : row + 1, :] for row in range(2)]
    put_rows(vecs, 4, (dshift, dscale, dcenter, dgain, doffset, *rest))
    if not isinstance(spread, Whole):
        share = vecs.shape[0] // spread.quarters
        for quarter in range(spread.quarters):
            spread.same(quarter, spread.rows - share, vecs[quarter * share : (quarter + 1) * share, :])
        where = (slice(None), slice(None), slice(spread.rows - share, spread.rows))
        io.send_part(spread.ref, PARTS - 1, where)


def small_kernel(body, name, outs, place, *args):
    vmem = pl.BlockSpec(memory_space=pltpu.VMEM)
    moved = sum(a.size * a.dtype.itemsize for a in (*args, *outs))
    return pl.pallas_call(
        body,
        out_shape=outs,
        in_specs=[pl.BlockSpec(memory_space=pltpu.SMEM)] + [vmem] * len(args),
        out_specs=[vmem] * len(outs),
        name=name,
        cost_estimate=pl.CostEstimate(flops=0, bytes_accessed=moved, transcendentals=0),
        compiler_params=pltpu.CompilerParams(vmem_limit_bytes=SMALL_BYTES),
    )(place, *args)


def split_kernel(pairs, extra, place_ref, *refs):
    outs = refs[2 * pairs + extra :]
    for step, out_ref in enumerate(outs):
        quarter = place_ref[7] ^ step
        at = 0
        for plane in range(refs[0].shape[1]):
            for pair in range(pairs):
                keep_ref, came_ref = refs[2 * pair : 2 * pair + 2]
                rows = keep_ref.shape[2]
                total = keep_ref[quarter, plane].astype(F32) + came_ref[quarter, plane].astype(F32)
                out_ref[at : at + rows, :] = total.astype(BF)
                at += rows
        if extra:
            out_ref[at:, :] = refs[2 * pairs][quarter]


def split_pieces(place, pairs, extra=None):
    quarters, planes, _, width = pairs[0][0].shape
    rows = planes * sum(keep.shape[2] for keep, _ in pairs)
    args = [part for pair in pairs for part in pair]
    if extra is not None:
        rows += extra.shape[1]
        args.append(extra)
    body = functools.partial(split_kernel, len(pairs), int(extra is not None))
    outs = [jax.ShapeDtypeStruct((rows, width), BF)] * quarters
    return list(small_kernel(body, "split", outs, place, *args))


def join_kernel(place_ref, whole_ref, pieces_ref, *outs):
    rows = whole_ref.shape[0]
    for step, out_ref in enumerate(outs):
        out_ref[:rows, :] = whole_ref[...]
        out_ref[rows:, :] = pieces_ref[place_ref[7] ^ step]


def join_pieces(place, whole, pieces):
    outs = [jax.ShapeDtypeStruct((whole.shape[0] + pieces.shape[1], whole.shape[1]), BF)] * pieces.shape[0]
    return list(small_kernel(join_kernel, "join", outs, place, whole, pieces))


def home_kernel(place_ref, *refs):
    dus, came_refs, outs = (refs[:2], refs[2:4]), refs[4:6], refs[6:]
    rows = outs[0].shape[1]
    for which, out_ref in enumerate(outs):
        at = pl.multiple_of((place_ref[9] ^ which) * rows, rows)
        for number, (du, came_ref) in enumerate(zip(dus, came_refs, strict=True)):
            out_ref[number] = (du[which][...].astype(F32) + came_ref[pl.ds(at, rows), :].astype(F32)).astype(BF)


def home_blocks(place, source_du, source_came, target_du, target_came):
    outs = [jax.ShapeDtypeStruct((2, *source_du[0].shape), BF)] * 2
    return list(small_kernel(home_kernel, "home", outs, place, *source_du, *target_du, source_came, target_came))


def fold_kernel(sets, planes, with_ready, place_ref, *refs):
    parts, outs = refs[:-planes], refs[-planes:]
    above = 0
    if with_ready:
        ready, parts = parts[-planes:], parts[:-planes]
        above = ready[0].shape[0]
    quarters, rows = len(parts) // sets, (outs[0].shape[0] - above) // sets
    for step, out_ref in enumerate(outs):
        if with_ready:
            out_ref[:above, :] = ready[step][...]
        plane = (place_ref[8] // 2) ^ step
        where = pl.ds(pl.multiple_of(plane * rows, rows), rows)
        for number in range(sets):
            of_set = parts[number * quarters : (number + 1) * quarters]
            total = sum(part[where, :].astype(F32) for part in of_set)
            at = above + number * rows
            out_ref[at : at + rows, :] = total.astype(BF)


def fold_pieces(place, sets, planes, height, ready=()):
    rows = len(sets) * height // planes + (ready[0].shape[0] if ready else 0)
    outs = [jax.ShapeDtypeStruct((rows, sets[0][0].shape[1]), BF)] * planes
    body = functools.partial(fold_kernel, len(sets), planes, bool(ready))
    return list(small_kernel(body, "fold", outs, place, *[part for parts in sets for part in parts], *ready))


def unpack_kernel(plan, io):
    chip, group = io.place[7], io.place[8]
    pieces = [ref for key, ref in io.small.items()]
    if len(pieces) == 1:
        pieces = [(quarter, pieces[0].at[quarter]) for quarter in range(pieces[0].shape[0])]
    else:
        pieces = [(chip ^ step, ref) for step, ref in enumerate(pieces)]
    quarters = len(pieces)
    for quarter, piece_ref in pieces:
        width = piece_ref.shape[1]
        at = 0
        for kind, outs in plan:
            refs = getattr(io, outs)
            if kind == ATTENTION:
                size = refs[0].shape[0] // quarters
                rows = pl.ds(pl.multiple_of(quarter * size, size), size)
                values = [piece_ref[at + i * size : at + (i + 1) * size, :].astype(F32) for i in range(4)]
                refs[0][rows, :] = values[0]
                refs[1][rows, :width] = values[1]
                refs[1][rows, width:] = values[2]
                refs[2][rows, :] = values[3]
                at += 4 * size
            elif kind == FEEDFORWARD:
                size = refs[0].shape[0]
                cols = pl.ds(pl.multiple_of(quarter * width, width), width)
                refs[0][:, cols] = piece_ref[at : at + size, :].astype(F32)
                at += size
                size = refs[1].shape[0] // quarters
                rows = pl.ds(pl.multiple_of(quarter * size, size), size)
                refs[1][rows, :] = piece_ref[at : at + size, :].astype(F32)
                at += size
            else:
                size = piece_ref.shape[0] - at
                rows = pl.ds(pl.multiple_of(quarter * size, size), size)
                refs[0][rows, :] = piece_ref[at:, :].astype(F32)
    if kind == VECTORS:
        short = refs[1].shape[0]
        pair = refs[0][:, pl.ds(pl.multiple_of((group // 2) * 2 * short, 2 * short), 2 * short)]
        thin = jnp.where(group % 2 == 0, pair[:, :short], pair[:, short:])
        for number, at in enumerate(THIN_ROWS):
            refs[1 + number][...] = thin[at]
        long = 4 * short
        lanes = pl.ds(pl.multiple_of((group % 2) * long, long), long)
        for number, at in enumerate(LONG_ROWS):
            refs[1 + len(THIN_ROWS) + number][...] = refs[0][pl.ds(at + group // 2, 1), lanes][0]


ATTENTION, FEEDFORWARD, VECTORS = range(3)
THIN_ROWS = (4, 5, 6, 7, 8, 13, 14, 15, 16, 17, 18, 19)
LONG_ROWS = (0, 9)


class Places:
    def __init__(self, quarters, groups):
        self.quarters, self.groups = quarters, groups
        self.sends = []
        for which in range(2):
            pairs = []
            for quarter in range(quarters):
                for group in range(groups):
                    plane, core = divmod(group, 2)
                    worker = self.chip_of(core, self.place_of(quarter) ^ which)
                    target = worker * groups + 2 * plane + self.group_of(quarter)
                    pairs.append((quarter * groups + group, target))
            self.sends.append(pairs)
        self.cores = [(group, group ^ 1) for group in range(groups)]

    def group_of(self, quarter):
        return (quarter ^ (quarter >> 1)) & 1

    def place_of(self, quarter):
        return quarter >> 1

    def chip_of(self, group, place):
        return 2 * place + (group ^ place)

    def order(self, rows, upper):
        return [jnp.where(upper, rows[1], rows[0]), jnp.where(upper, rows[0], rows[1])]

    def to_work(self, parts):
        return [
            lax.ppermute(part, ("pipe", "dp"), pairs)
            for part, pairs in zip(parts, self.sends, strict=True)
        ]

    def to_home(self, block_a, block_b):
        return [
            lax.ppermute(part, ("pipe", "dp"), pairs)
            for part, pairs in zip((block_a, block_b), self.sends, strict=True)
        ]

    def at_home(self, came, upper):
        first, second = came
        return jnp.stack([jnp.where(upper, second, first), jnp.where(upper, first, second)])

    def to_other_core(self, value):
        return lax.ppermute(value, "dp", self.cores)


def gate(*values):
    return list(lax.optimization_barrier(values))


def together(*values):
    return lax.optimization_barrier(values)


def after(results, *flying):
    kept, flying = lax.optimization_barrier((dict(results), flying))
    return Results(kept), *flying


def to_quarters(parts):
    quarters = len(parts)
    return [
        part if step == 0 else lax.ppermute(part, "pipe", [(i, i ^ step) for i in range(quarters)])
        for step, part in enumerate(parts)
    ]


def to_planes(parts):
    groups = 2 * len(parts)
    return [
        part if step == 0 else lax.ppermute(part, "dp", [(i, i ^ (2 * step)) for i in range(groups)])
        for step, part in enumerate(parts)
    ]


def total_of(parts):
    return sum(part.astype(F32) for part in parts).astype(BF)


def by_step(value, index):
    return [
        lax.dynamic_index_in_dim(value, index ^ step, 0, keepdims=False) for step in range(value.shape[0])
    ]


def shards(
    source, target, source_length, target_length, memory_cotangent, output_cotangent,
    source_query, source_keyvalue, source_output, source_gain, source_offset,
    source_expand, source_bias, source_contract, source_shift, source_scale, source_center,
    target_query, target_keyvalue, target_output, target_gain, target_offset,
    cross_query, cross_keyvalue, cross_output, cross_gain, cross_offset,
    target_expand, target_bias, target_contract, target_shift, target_scale, target_center,
):
    quarters, groups = lax.axis_size("pipe"), lax.axis_size("dp")
    chip, group = lax.axis_index("pipe"), lax.axis_index("dp")
    core, planes = group % 2, groups // 2
    micro, block, width = source.shape
    rows, keys = 2 * block, 4 * block
    heads = width // HEAD_DIM
    wide = source_expand.shape[1]
    spread = (width // groups) % (16 * quarters) == 0
    places = Places(quarters, groups)
    upper = chip >= quarters // 2
    swap = places.to_other_core

    lengths = jnp.stack([source_length, target_length])
    other_lengths = swap(lengths)
    own = places.to_work(places.order(source, upper))
    counts = jnp.where(core == places.group_of(chip), lengths, other_lengths)
    counts = lax.dynamic_index_in_dim(counts, places.place_of(chip), 1, keepdims=False)
    starts = [places.chip_of(which, at) * block for which in (core, 1 - core) for at in range(2)]
    slots = [*starts, counts[0], counts[1], core, chip, group, places.place_of(chip)]
    place = jnp.stack([jnp.asarray(slot, jnp.int32) for slot in slots])
    late = places.order(jnp.stack([target, output_cotangent, memory_cotangent], 1), upper)
    own, late, place = together(own, late, place)
    other = Ends(swap(part) for part in own)
    own = Ends(own)
    late = places.to_work(late)


    def row(vector):
        return vector.reshape(1, -1)

    def shape(*dims, dtype=BF):
        return jax.ShapeDtypeStruct(dims, dtype)

    half = shape(block, width)
    sheet = shape(rows, width, dtype=F32)
    lanes = shape(rows, 128, dtype=F32)
    saved = Results(
        q=shape(rows, width), k=shape(keys, width), v=shape(keys, width),
        ot=shape(width, rows, dtype=F32), lse=shape(heads, rows, dtype=F32),
    )
    flat_bias = pltpu.VMEM((keys, 128), F32)
    causal_bias = pltpu.VMEM((keys, rows), F32)
    back_scratch = [
        pltpu.VMEM((rows, width), BF), pltpu.VMEM((heads, rows), F32), pltpu.VMEM((width, rows), BF),
        pltpu.VMEM((keys, width), BF), pltpu.VMEM((keys, width), BF),
    ]
    vec_rows = 16 * quarters
    if spread:
        attn_rows = 4 * width // (groups * quarters)
        ffn_rows = 2 * wide // (groups * quarters)
        attention_grads = [shape(quarters, planes, attn_rows, width)] * 2
        top_grads = shape(groups, quarters, ffn_rows, width)
        source_ffn_grads = shape(groups, quarters, ffn_rows + vec_rows // quarters, width)
    else:
        attention_grads = [shape(width, cols) for cols in (width, 2 * width, width)]
        top_grads = [shape(width, wide), shape(wide, width), shape(16, 128)]
        source_ffn_grads = top_grads
    core_flops = 2 * 4 * rows * keys * width
    linear_flops = 2 * rows * width * width
    ffn_flops = 4 * rows * width * wide
    attn_flops = 2 * core_flops + 8 * linear_flops
    attn_back_flops = 5 * core_flops + 16 * linear_flops

    encoder = run(
        encoder_forward_kernel, "encoder", attn_flops + ffn_flops, place,
        dict(own=own, wq=source_query, other=other, wkv=source_keyvalue, rest=None, wo=source_output, w1=source_expand,
             w2=source_contract),
        dict(gain=row(source_gain), offset=row(source_offset), b1=row(source_bias), b2=row(source_shift),
             scale=row(source_scale), center=row(source_center)),
        dict(**saved, n0=sheet, i0=lanes, hidden=shape(rows, width), active=shape(rows, wide),
             slope=shape(rows, wide), n1=sheet, i1=lanes, memory=shape(rows, width)),
        [flat_bias],
    )
    *late, memory = gate(*late, encoder.memory)
    target_own = Ends((part, 0) for part in late)
    target_other = Ends(swap(part[0]) for part in late)
    memory_other = swap(memory)
    top = run(
        decoder_forward_kernel, "decoder", 2 * attn_flops + 3 * ffn_flops, place,
        dict(sown=target_own, swq=target_query, sother=target_other, swkv=target_keyvalue, rest=None, swo=target_output,
             wq=cross_query, mem_own=memory, mem_other=memory_other, wkv=cross_keyvalue, wo=cross_output,
             w1=target_expand, w2=target_contract, cotangent=Ends((part, 1) for part in late)),
        dict(gain=row(target_gain), offset=row(target_offset), cross_gain=row(cross_gain),
             cross_offset=row(cross_offset), b1=row(target_bias), b2=row(target_shift), scale=row(target_scale),
             center=row(target_center)),
        dict(sq=saved.q, sk=saved.k, sv=saved.v, sot=saved.ot, slse=saved.lse, n=sheet, i=lanes, **saved,
             first=shape(rows, width), result=Ends([shape(2, block, width)] * 2), dr=sheet, dv=sheet,
             vecs=shape(16, width, dtype=F32), grads=top_grads),
        [causal_bias, flat_bias, pltpu.VMEM((rows, wide), BF), pltpu.VMEM((rows, wide), BF)],
    )
    results = places.to_home(*top.result)
    if spread:
        top_total = lax.psum_scatter(top.grads, "dp", scatter_dimension=0, tiled=True)[0]

    def kept(results):
        return dict(ot=results.ot, k=results.k, q=results.q, v=results.v, lse=results.lse, rest=None)

    decoder = Results(ot=top.sot, k=top.sk, q=top.sq, v=top.sv, lse=top.slse)

    cross = run(
        cross_backward_kernel, "cross_back", attn_back_flops, place,
        dict(dv=top.dv, wo=cross_output, **kept(top), first=top.first, mem_own=memory, mem_other=memory_other,
             wkv=cross_keyvalue, wq=cross_query, n=top.n, i=top.i),
        dict(gain=row(target_gain)),
        dict(dmem_own=shape(rows, width), dmem_other=shape(rows, width), dv1=sheet, vecs=shape(8, width, dtype=F32),
             grads=attention_grads),
        [flat_bias, *back_scratch],
    )
    cross, results = after(cross, results)
    results = places.at_home(results, upper)
    dmem_came = swap(cross.dmem_other)
    cross_came = swap(cross.grads[1]) if spread else ()
    target_back = run(
        target_backward_kernel, "target_back", attn_back_flops, place,
        dict(dv=cross.dv1, wo=target_output, **kept(decoder), own=target_own, other=target_other,
             wkv=target_keyvalue, wq=target_query, extra=top.dr),
        {}, dict(dc_other=shape(rows, width), du=Ends([half, half]), grads=attention_grads),
        [causal_bias, *back_scratch],
    )
    target_back, dmem_came, cross_came = after(target_back, dmem_came, cross_came)
    dtarget_came = swap(target_back.dc_other)
    target_came, early = (), ()
    if spread:
        target_came = swap(target_back.grads[1])
        early = split_pieces(place, [(cross.grads[0], cross_came)])
        early, dmem_came = together(early, dmem_came)
        early = to_quarters(early)
    source_ffn = run(
        encoder_ffn_backward, "source_ffn", 2 * ffn_flops, place,
        dict(cotangent=Ends((part, 2) for part in late), dmem_own=cross.dmem_own, dmem_came=dmem_came,
             n1=encoder.n1, i1=encoder.i1, w2=Blocks(source_contract, 0), slope=Blocks(encoder.slope, 1),
             w1=Blocks(source_expand, 1), active=Blocks(encoder.active, 1), hidden=encoder.hidden, n0=encoder.n0,
             i0=encoder.i0),
        dict(scale=row(source_scale), gain=row(source_gain), top_vecs=top.vecs, cross_vecs=cross.vecs),
        dict(dr=sheet, dv=sheet, vecs=shape(vec_rows, width, dtype=F32), grads=source_ffn_grads),
    )
    source_ffn, dtarget_came, target_came, early = after(source_ffn, dtarget_came, target_came, early)
    dv0, middle = source_ffn.dv, ()
    if spread:
        source_total = lax.psum_scatter(source_ffn.grads, "dp", scatter_dimension=0, tiled=True)[0]
        middle = split_pieces(place, [(target_back.grads[0], target_came)], top_total)
        dv0, middle = together(dv0, middle)
        middle = to_quarters(middle)
    source_back = run(
        source_backward_kernel, "source_back", attn_back_flops, place,
        dict(dv=dv0, wo=source_output, **kept(encoder), own=own, other=other, wkv=source_keyvalue,
             wq=source_query, extra=source_ffn.dr),
        {}, dict(dc_other=shape(rows, width), du=Ends([half, half]), grads=attention_grads),
        [flat_bias, *back_scratch],
    )
    source_back, middle = after(source_back, middle)

    def attention_outs():
        chunk = width // groups
        return [shape(chunk, width, dtype=F32), shape(chunk, 2 * width, dtype=F32), shape(chunk, width, dtype=F32)]

    def ffn_outs():
        return [shape(width // groups, wide, dtype=F32), shape(wide // groups, width, dtype=F32)]

    def unpack(name, plan, parts, outs):
        return run(
            functools.partial(unpack_kernel, plan), name, 0, place, {}, dict(enumerate(parts)), outs, vmem_bytes=SMALL_BYTES
        )

    dc_other = source_back.dc_other
    if spread:
        last_came = swap(source_back.grads[1])
        last = split_pieces(place, [(source_back.grads[0], last_came)])
        height = planes * attn_rows
        home = home_blocks(place, source_back.du, swap(dc_other), target_back.du, dtarget_came)
        last, home = together(last, home)
        last, home = to_quarters(last), places.to_home(*home)
        first = total_of([part[height:] for part in middle])
        ready = fold_pieces(place, [early, middle], planes, height)
        both = to_planes(fold_pieces(place, [last], planes, height, ready))
        pieces = to_quarters(join_pieces(place, first, source_total))
        both, pieces, home = together(both, pieces, home)
        first = pieces
        pieces = [part[ffn_rows:] for part in pieces]
        last = [jnp.concatenate([total_of(both), total_of(pieces)], 0)] * quarters
        last = to_quarters(last)
    else:
        home = home_blocks(place, source_back.du, swap(dc_other), target_back.du, dtarget_came)
        home = places.to_home(*home)
    gradients = places.at_home(home, upper).astype(F32)
    if spread:
        first_grads = unpack(
            "unpack_first", ((FEEDFORWARD, "top"),), first, dict(top=ffn_outs()),
        )
        last_grads = unpack(
            "unpack_last",
            (
                (ATTENTION, "cross"), (ATTENTION, "target"), (ATTENTION, "source"), (FEEDFORWARD, "low"),
                (VECTORS, "vectors"),
            ),
            last,
            dict(cross=attention_outs(), target=attention_outs(), source=attention_outs(), low=ffn_outs(),
                 vectors=[shape(vec_rows, width, dtype=F32)] + [shape(width // groups, dtype=F32)] * len(THIN_ROWS)
                 + [shape(wide // groups, dtype=F32)] * len(LONG_ROWS)),
        )
        thin = dict(zip(THIN_ROWS, last_grads.vectors[1:], strict=False))
        biases = dict(zip(LONG_ROWS, last_grads.vectors[-len(LONG_ROWS) :], strict=True))
        source_attn, target_attn, cross_attn = last_grads.source, last_grads.target, last_grads.cross
        source_wide, target_wide = last_grads.low, first_grads.top
    else:
        vectors = lax.psum(source_ffn.vecs, ("pipe", "dp"))
        thin = lax.dynamic_slice_in_dim(vectors, group * (width // groups), width // groups, 1)

        def reduced(parts):
            flat = jnp.concatenate([part.reshape(groups, -1) for part in parts], 1)
            total = lax.psum(lax.psum_scatter(flat, "dp", scatter_dimension=0, tiled=True)[0], "pipe")
            outs, at = [], 0
            for part in parts:
                size = part.size // groups
                outs.append(total[at : at + size].reshape(-1, part.shape[1]).astype(F32))
                at += size
            return outs

        source_attn, target_attn, cross_attn = [
            reduced(results.grads) for results in (source_back, target_back, cross)
        ]
        source_wide, target_wide = [reduced(results.grads[:2]) for results in (source_ffn, top)]

    def bias(first_row):
        if spread:
            return biases[first_row]
        whole = vectors[first_row : first_row + wide // width].reshape(groups, -1)
        return lax.dynamic_index_in_dim(whole, group, 0, keepdims=False)

    return (
        results[:, 0], results[:, 1], gradients[:, 0], gradients[:, 1],
        *source_attn, thin[7], thin[8],
        source_wide[0], bias(0), source_wide[1], thin[4], thin[5], thin[6],
        *target_attn, thin[18], thin[19],
        *cross_attn, thin[16], thin[17],
        target_wide[0], bias(9), target_wide[1], thin[13], thin[14], thin[15],
    )


def solution(mesh):
    rows = P("dp", "pipe", None)
    matrix, vector = P("dp", None), P("dp")
    in_specs = (rows, rows, P("dp"), P("dp"), rows, rows) + (P(),) * 27
    attention = (matrix, matrix, matrix, vector, vector)
    ffn = (matrix, vector, matrix, vector, vector, vector)
    out_specs = (rows,) * 4 + attention + ffn + attention + attention + ffn
    return jax.shard_map(shards, mesh=mesh, in_specs=in_specs, out_specs=out_specs, check_vma=False)
```

profile of v0, /device:TPU:0, one launch (start us, length us, event | category | flops | bytes accessed | tf_op | source)
XLA Modules:
  0.0 256.4 jit_solution(7101005711874279695)
XLA Ops:
  8.4 1.1 select_bitcast_fusion.6
  9.5 3.5 %collective-permute-start.1 = (bf16[256,512]{1,0:T(8,128)(2,1)S(1)}, bf16[256,512]{1,0:T(8,128)(2,1)S(1)}, u32[]{:S(2)}, u32[]{:S(2)}) collective-permute-start(bf16[256,512]{1,0:T(8,128)(2,1)S(1)} %get-tuple-element.383), channel_id=1, source_target_pairs={{0,24},{1,16},{2,26},{3,18},{4,28},{5,20},{6,30},{7,22},{8,25},{9,... | collective-permute-start | bytes 786440 | tf_op jit(solution)/shard_map/ppermute | solution.py:918
  13.0 1.4 collective-permute-start
  14.3 1.5 pad_maximum_fusion
  17.2 1.9 stack.81.place_ref
  19.1 1.4 collective-permute-start.5
  21.3 1.7 collective-permute-start.4
  23.8 20.2 %encoder.1 = (bf16[512,512]{1,0:T(8,128)(2,1)}, bf16[1024,512]{1,0:T(8,128)(2,1)}, bf16[1024,512]{1,0:T(8,128)(2,1)}, f32[512,512]{1,0:T(8,128)}, f32[8,512]{1,0...) custom-call(s32[10]{0:T(128)} %stack.81.place_ref, ...), custom_call_target="tpu_custom_call" | custom-call | flops 8589934592 | bytes 18890752 | tf_op jit(solution)/shard_map/encoder/pallas_call | solution.py:511
  44.0 2.1 collective-permute-start.9
  46.7 1.3 collective-permute-done.8.refs_12_.refs_10_
  49.3 35.0 %decoder.1 = (bf16[512,512]{1,0:T(8,128)(2,1)}, bf16[1024,512]{1,0:T(8,128)(2,1)}, bf16[1024,512]{1,0:T(8,128)(2,1)}, f32[512,512]{1,0:T(8,128)}, f32[8,512]{1,0...) custom-call(s32[10]{0:T(128)} %stack.81.place_ref, ...), custom_call_target="tpu_custom_call" | custom-call | flops 19327352832 | bytes 29687808 | tf_op jit(solution)/shard_map/decoder/pallas_call | solution.py:511
  84.4 0.9 copy-done.25
  86.3 1.5 collective-permute-start.11
  87.8 20.2 %cross_back.1 = (bf16[512,512]{1,0:T(8,128)(2,1)}, bf16[512,512]{1,0:T(8,128)(2,1)}, f32[512,512]{1,0:T(8,128)}, f32[8,512]{1,0:T(8,128)}, bf16[4,4,64,512]{3,2,...) custom-call(s32[10]{0:T(128)} %stack.81.place_ref, f32[1,512]{1,0:T(1,128)} %bitcast.80, ...), custom_call_target="tpu_custom_call" | custom-call | flops 15032385536 | bytes 13926400 | tf_op jit(solution)/shard_map/cross_back/pallas_call | solution.py:511
  108.0 2.3 collective-permute-start.12
  110.5 16.6 %target_back.1 = (bf16[512,512]{1,0:T(8,128)(2,1)}, bf16[256,512]{1,0:T(8,128)(2,1)}, bf16[256,512]{1,0:T(8,128)(2,1)}, bf16[4,4,64,512]{3,2,1,0:T(8,128)(2,1)}, bf16[4,4,64,512]{3,2,1,0:T(8,128)(2,1)}) custom-call(s32[10]{0:T(128)} %stack.81.place_ref, f32[512,512]{1,0:T(8,128)} %get-tuple-element.234.refs_0_, bf16[512,512]{1,0:T(8,128)(2,1)} %refs_1_.2, ...), custom_call_target="tpu_custom_call" | custom-call | flops 15032385536 | bytes 13123584 | tf_op jit(solution)/shard_map/target_back/pallas_call | solution.py:511
  128.7 2.2 collective-permute-start.16
  130.9 1.5 collective-permute-start.18
  132.4 13.7 %source_ffn.1 = (f32[512,512]{1,0:T(8,128)}, f32[512,512]{1,0:T(8,128)}, f32[64,512]{1,0:T(8,128)}, bf16[8,4,144,512]{3,2,1,0:T(8,128)(2,1)}) custom-call(s32[10]{0:T(128)} %stack.81.place_ref, f32[1,512]{1,0:T(1,128)} %bitcast.84, f32[1,512]{1,0:T(1,128)} %bitcast.82, f32[16,512]{1,0:T(8,128)} %get-tuple-element.230.refs_2_, ...), custom_call_target="tpu_custom_call" | custom-call | flops 4294967296 | bytes 21102592 | tf_op jit(solution)/shard_map/source_ffn/pallas_call | solution.py:511
  146.9 1.2 copy-done.2
  148.1 1.0 copy-done.4
  149.9 2.0 collective-permute-start.19
  151.9 1.5 collective-permute-start.21
  153.5 19.3 %source_back.1 = (bf16[512,512]{1,0:T(8,128)(2,1)}, bf16[256,512]{1,0:T(8,128)(2,1)}, bf16[256,512]{1,0:T(8,128)(2,1)}, bf16[4,4,64,512]{3,2,1,0:T(8,128)(2,1)}, bf16[4,4,64,512]{3,2,1,0:T(8,128)(2,1)}) custom-call(s32[10]{0:T(128)} %stack.81.place_ref, f32[512,512]{1,0:T(8,128)} %get-tuple-element.279.refs_0_, bf16[512,512]{1,0:T(8,128)(2,1)} %refs_1_.3, ...), custom_call_target="tpu_custom_call" | custom-call | flops 15032385536 | bytes 12075008 | tf_op jit(solution)/shard_map/source_back/pallas_call | solution.py:511
  173.4 3.2 %collective-permute-done.23.refs_4_ = bf16[512,512]{1,0:T(8,128)(2,1)S(1)} collective-permute-done((bf16[512,512]{1,0:T(8,128)(2,1)}, bf16[512,512]{1,0:T(8,128)(2,1)S(1)}, u32[]{:S(2)}, u32[]{:S(2)}) %collective-permute-start.23) | collective-permute-done | bytes 524320 | tf_op jit(solution)/shard_map/ppermute | solution.py:933
  180.2 2.0 collective-permute-start.24
  182.5 1.2 collective-permute-start.26
  185.4 1.7 collective-permute-start.34
  187.2 2.2 collective-permute-done.24.refs_1_
  189.4 7.0 %collective-permute-done.25.refs_2_ = bf16[256,512]{1,0:T(8,128)(2,1)S(1)} collective-permute-done((bf16[256,512]{1,0:T(8,128)(2,1)S(1)}, bf16[256,512]{1,0:T(8,128)(2,1)S(1)}, u32[]{:S(2)}, u32[]{:S(2)}) %collective-permute-start.25) | collective-permute-done | bytes 262176 | tf_op jit(solution)/shard_map/ppermute | solution.py:952
  197.1 1.4 collective-permute-start.27
  198.5 2.7 %collective-permute-start.28 = (bf16[192,512]{1,0:T(8,128)(2,1)S(1)}, bf16[192,512]{1,0:T(8,128)(2,1)}, u32[]{:S(2)}, u32[]{:S(2)}) collective-permute-start(bf16[192,512]{1,0:T(8,128)(2,1)S(1)} %get-tuple-element.327), channel_id=1, source_target_pairs={{0,4},{1,5},{2,6},{3,7},{4,0},{5,1},{6,2},{7,3},{8,12},{9,13},{10,... | collective-permute-start | bytes 589832 | tf_op jit(solution)/shard_map/ppermute | solution.py:960
  201.6 2.1 reduce-scatter.5.cloned.1.call-done
  203.7 1.1 copy-done.3
  205.4 2.9 %collective-permute-done.27 = bf16[192,512]{1,0:T(8,128)(2,1)} collective-permute-done((bf16[192,512]{1,0:T(8,128)(2,1)S(1)}, bf16[192,512]{1,0:T(8,128)(2,1)}, u32[]{:S(2)}, u32[]{:S(2)}) %collective-permute-start.27) | collective-permute-done | bytes 196640 | tf_op jit(solution)/shard_map/ppermute | solution.py:960
  208.3 1.4 collective-permute-start.30
  209.7 6.1 %collective-permute-done.28 = bf16[192,512]{1,0:T(8,128)(2,1)} collective-permute-done((bf16[192,512]{1,0:T(8,128)(2,1)S(1)}, bf16[192,512]{1,0:T(8,128)(2,1)}, u32[]{:S(2)}, u32[]{:S(2)}) %collective-permute-start.28) | collective-permute-done | bytes 196640 | tf_op jit(solution)/shard_map/ppermute | solution.py:960
  215.8 1.1 collective-permute-start.31
  216.8 2.0 collective-permute-start.32
  218.9 1.1 fusion.2
  220.0 11.0 %collective-permute-done.31.refs_2_ = bf16[272,512]{1,0:T(8,128)(2,1)S(1)} collective-permute-done((bf16[272,512]{1,0:T(8,128)(2,1)S(1)}, bf16[272,512]{1,0:T(8,128)(2,1)S(1)}, u32[]{:S(2)}, u32[]{:S(2)}) %collective-permute-start.31) | collective-permute-done | bytes 278560 | tf_op jit(solution)/shard_map/ppermute | solution.py:952
  231.1 1.2 add_convert_fusion
  232.3 3.1 %collective-permute-start.37 = (bf16[336,512]{1,0:T(8,128)(2,1)S(1)}, bf16[336,512]{1,0:T(8,128)(2,1)S(1)}, u32[]{:S(2)}, u32[]{:S(2)}) collective-permute-start(bf16[336,512]{1,0:T(8,128)(2,1)S(1)} %pad_maximum_fusion.2.refs_0_), channel_id=1, source_target_pairs={{0,24},{8,16},{16,8},{24,0},{1,25},{9,17},{17,9},{25,1},{2,26},{10... | collective-permute-start | bytes 1032200 | tf_op jit(solution)/shard_map/ppermute | solution.py:952
  236.1 1.2 select_bitcast_fusion.3
  237.4 1.8 unpack_first.1
  239.2 1.5 slice_bitcast_fusion
  240.7 3.6 %collective-permute-done.36.refs_2_ = bf16[336,512]{1,0:T(8,128)(2,1)S(1)} collective-permute-done((bf16[336,512]{1,0:T(8,128)(2,1)S(1)}, bf16[336,512]{1,0:T(8,128)(2,1)S(1)}, u32[]{:S(2)}, u32[]{:S(2)}) %collective-permute-start.36) | collective-permute-done | bytes 344096 | tf_op jit(solution)/shard_map/ppermute | solution.py:952
  244.3 5.0 %unpack_last.1 = (f32[64,512]{1,0:T(8,128)}, f32[64,1024]{1,0:T(8,128)}, f32[64,512]{1,0:T(8,128)}, f32[64,512]{1,0:T(8,128)}, f32[64,1024]{1,0:T(8,128)}, /*ind...) custom-call(s32[10]{0:T(128)S(1)} %copy-done.13, ...), custom_call_target="tpu_custom_call" | custom-call | bytes 2757632 | tf_op jit(solution)/shard_map/unpack_last/pallas_call | solution.py:511
  (130 shorter events, 19.0 us)
Async XLA Ops:
  7.2 139.7 %reduce-scatter.3.cloned.1.call-start = ((), (), s32[]{:S(2)}) async-start(), calls=%async_computation.2 | async-start | bytes 4718592 | tf_op jit(solution)/shard_map/reduce_scatter | solution.py:1075
  7.9 8.1 %collective-permute-start.2 = (s32[2,2]{1,0:T(2,128)S(1)}, s32[2,2]{1,0:T(2,128)S(1)}, u32[]{:S(2)}, u32[]{:S(2)}) collective-permute-start(s32[2,2]{1,0:T(2,128)S(1)} %pad_add_fusion), channel_id=1, source_target_pairs={{0,1},{1,0},{2,3},{3,2},{4,5},{5,4},{6,7},{7,6},{8,9},{9,8},{10,11... | collective-permute-start | bytes 56 | tf_op jit(solution)/shard_map/ppermute | solution.py:933
  9.5 9.6 %collective-permute-start.1 = (bf16[256,512]{1,0:T(8,128)(2,1)S(1)}, bf16[256,512]{1,0:T(8,128)(2,1)S(1)}, u32[]{:S(2)}, u32[]{:S(2)}) collective-permute-start(bf16[256,512]{1,0:T(8,128)(2,1)S(1)} %get-tuple-element.383), channel_id=1, source_target_pairs={{0,24},{1,16},{2,26},{3,18},{4,28},{5,20},{6,30},{7,22},{8,25},{9,... | collective-permute-start | bytes 786440 | tf_op jit(solution)/shard_map/ppermute | solution.py:918
  13.0 6.1 %collective-permute-start = (bf16[256,512]{1,0:T(8,128)(2,1)S(1)}, bf16[256,512]{1,0:T(8,128)(2,1)}, u32[]{:S(2)}, u32[]{:S(2)}) collective-permute-start(bf16[256,512]{1,0:T(8,128)(2,1)S(1)} %get-tuple-element.384), channel_id=1, source_target_pairs={{0,0},{1,8},{2,2},{3,10},{4,4},{5,12},{6,6},{7,14},{8,1},{9,9},{10... | collective-permute-start | bytes 786440 | tf_op jit(solution)/shard_map/ppermute | solution.py:918
  19.1 3.9 %collective-permute-start.5 = (bf16[256,512]{1,0:T(8,128)(2,1)}, bf16[256,512]{1,0:T(8,128)(2,1)S(1)}, u32[]{:S(2)}, u32[]{:S(2)}) collective-permute-start(bf16[256,512]{1,0:T(8,128)(2,1)} %collective-permute-done.refs_6_.refs_7_), channel_id=1, source_target_pairs={{0,1},{1,0},{2,3},{3,2},{4,5},{5,4},{6,7},{7,6},{8,9},{9,8},{10,11... | collective-permute-start | bytes 786440 | tf_op jit(solution)/shard_map/ppermute | solution.py:933
  20.5 2.5 collective-permute-start.6
  20.6 23.4 %collective-permute-start.3 = (bf16[3,256,512]{2,1,0:T(8,128)(2,1)S(1)}, bf16[3,256,512]{2,1,0:T(8,128)(2,1)S(1)}, u32[]{:S(2)}, u32[]{:S(2)}) collective-permute-start(bf16[3,256,512]{2,1,0:T(8,128)(2,1)S(1)} %get-tuple-element.203), channel_id=1, source_target_pairs={{0,0},{1,8},{2,2},{3,10},{4,4},{5,12},{6,6},{7,14},{8,1},{9,9},{10... | collective-permute-start | bytes 2359304 | tf_op jit(solution)/shard_map/ppermute | solution.py:918
  21.3 22.7 %collective-permute-start.4 = (bf16[3,256,512]{2,1,0:T(8,128)(2,1)S(1)}, bf16[3,256,512]{2,1,0:T(8,128)(2,1)S(1)}, u32[]{:S(2)}, u32[]{:S(2)}) collective-permute-start(bf16[3,256,512]{2,1,0:T(8,128)(2,1)S(1)} %get-tuple-element.204), channel_id=1, source_target_pairs={{0,24},{1,16},{2,26},{3,18},{4,28},{5,20},{6,30},{7,22},{8,25},{9,... | collective-permute-start | bytes 2359304 | tf_op jit(solution)/shard_map/ppermute | solution.py:918
  44.0 4.4 %collective-permute-start.9 = (bf16[512,512]{1,0:T(8,128)(2,1)}, bf16[512,512]{1,0:T(8,128)(2,1)S(1)}, u32[]{:S(2)}, u32[]{:S(2)}) collective-permute-start(bf16[512,512]{1,0:T(8,128)(2,1)} %get-tuple-element.210.refs_16_.refs_9_), channel_id=1, source_target_pairs={{0,1},{1,0},{2,3},{3,2},{4,5},{5,4},{6,7},{7,6},{8,9},{9,8},{10,11... | collective-permute-start | bytes 1572872 | tf_op jit(solution)/shard_map/ppermute | solution.py:933
  46.1 1.9 collective-permute-start.8
  46.2 2.2 collective-permute-start.7
  84.3 119.4 %reduce-scatter.5.cloned.1.call-start = ((), (), s32[]{:S(2)}) async-start(), calls=%async_computation.3 | async-start | bytes 5308416 | tf_op jit(solution)/shard_map/reduce_scatter | solution.py:1122
  85.3 22.7 %collective-permute-start.10 = (bf16[2,256,512]{2,1,0:T(8,128)(2,1)S(1)}, bf16[2,256,512]{2,1,0:T(8,128)(2,1)S(1)}, u32[]{:S(2)}, u32[]{:S(2)}) collective-permute-start(bf16[2,256,512]{2,1,0:T(8,128)(2,1)S(1)} %copy-done.25), channel_id=1, source_target_pairs={{0,0},{1,8},{2,2},{3,10},{4,4},{5,12},{6,6},{7,14},{8,1},{9,9},{10... | collective-permute-start | bytes 1572872 | tf_op jit(solution)/shard_map/ppermute | solution.py:924
  86.3 21.8 %collective-permute-start.11 = (bf16[2,256,512]{2,1,0:T(8,128)(2,1)S(1)}, bf16[2,256,512]{2,1,0:T(8,128)(2,1)S(1)}, u32[]{:S(2)}, u32[]{:S(2)}) collective-permute-start(bf16[2,256,512]{2,1,0:T(8,128)(2,1)S(1)} %copy-done.24), channel_id=1, source_target_pairs={{0,24},{1,16},{2,26},{3,18},{4,28},{5,20},{6,30},{7,22},{8,25},{9,... | collective-permute-start | bytes 1572872 | tf_op jit(solution)/shard_map/ppermute | solution.py:924
  108.0 19.0 %collective-permute-start.12 = (bf16[512,512]{1,0:T(8,128)(2,1)}, bf16[512,512]{1,0:T(8,128)(2,1)S(1)}, u32[]{:S(2)}, u32[]{:S(2)}) collective-permute-start(bf16[512,512]{1,0:T(8,128)(2,1)} %get-tuple-element.246), channel_id=1, source_target_pairs={{0,1},{1,0},{2,3},{3,2},{4,5},{5,4},{6,7},{7,6},{8,9},{9,8},{10,11... | collective-permute-start | bytes 1572872 | tf_op jit(solution)/shard_map/ppermute | solution.py:933
  110.4 16.7 %collective-permute-start.13 = (bf16[4,4,64,512]{3,2,1,0:T(8,128)(2,1)}, bf16[4,4,64,512]{3,2,1,0:T(8,128)(2,1)S(1)}, u32[]{:S(2)}, u32[]{:S(2)}) collective-permute-start(bf16[4,4,64,512]{3,2,1,0:T(8,128)(2,1)} %get-tuple-element.247), channel_id=1, source_target_pairs={{0,1},{1,0},{2,3},{3,2},{4,5},{5,4},{6,7},{7,6},{8,9},{9,8},{10,11... | collective-permute-start | bytes 3145736 | tf_op jit(solution)/shard_map/ppermute | solution.py:933
  110.5 17.4 %copy-start = (bf16[4,4,64,512]{3,2,1,0:T(8,128)(2,1)S(1)}, bf16[4,4,64,512]{3,2,1,0:T(8,128)(2,1)}, u32[]{:S(2)}) copy-start(bf16[4,4,64,512]{3,2,1,0:T(8,128)(2,1)} %get-tuple-element.233.refs_0_) | copy-start | bytes 3145732
  110.5 17.4 %copy-start.11 = (s32[10]{0:T(128)S(1)}, s32[10]{0:T(128)}, u32[]{:S(2)}) copy-start(s32[10]{0:T(128)} %stack.81.place_ref) | copy-start | bytes 124
  127.1 19.8 %collective-permute-start.15 = (bf16[4,4,64,512]{3,2,1,0:T(8,128)(2,1)}, bf16[4,4,64,512]{3,2,1,0:T(8,128)(2,1)S(1)}, u32[]{:S(2)}, u32[]{:S(2)}) collective-permute-start(bf16[4,4,64,512]{3,2,1,0:T(8,128)(2,1)} %get-tuple-element.266), channel_id=1, source_target_pairs={{0,1},{1,0},{2,3},{3,2},{4,5},{5,4},{6,7},{7,6},{8,9},{9,8},{10,11... | collective-permute-start | bytes 3145736 | tf_op jit(solution)/shard_map/ppermute | solution.py:933
  127.8 19.0 %collective-permute-start.14 = (bf16[512,512]{1,0:T(8,128)(2,1)}, bf16[512,512]{1,0:T(8,128)(2,1)S(1)}, u32[]{:S(2)}, u32[]{:S(2)}) collective-permute-start(bf16[512,512]{1,0:T(8,128)(2,1)} %get-tuple-element.265), channel_id=1, source_target_pairs={{0,1},{1,0},{2,3},{3,2},{4,5},{5,4},{6,7},{7,6},{8,9},{9,8},{10,11... | collective-permute-start | bytes 1572872 | tf_op jit(solution)/shard_map/ppermute | solution.py:933
  128.7 17.4 %collective-permute-start.16 = (bf16[256,512]{1,0:T(8,128)(2,1)S(1)}, bf16[256,512]{1,0:T(8,128)(2,1)S(1)}, u32[]{:S(2)}, u32[]{:S(2)}) collective-permute-start(bf16[256,512]{1,0:T(8,128)(2,1)S(1)} %get-tuple-element.268), channel_id=1, source_target_pairs={{0,8},{8,0},{16,24},{24,16},{1,9},{9,1},{17,25},{25,17},{2,10},{10... | collective-permute-start | bytes 786440 | tf_op jit(solution)/shard_map/ppermute | solution.py:952
  130.9 15.2 %collective-permute-start.17 = (bf16[256,512]{1,0:T(8,128)(2,1)S(1)}, bf16[256,512]{1,0:T(8,128)(2,1)S(1)}, u32[]{:S(2)}, u32[]{:S(2)}) collective-permute-start(bf16[256,512]{1,0:T(8,128)(2,1)S(1)} %get-tuple-element.269), channel_id=1, source_target_pairs={{0,16},{8,24},{16,0},{24,8},{1,17},{9,25},{17,1},{25,9},{2,18},{10... | collective-permute-start | bytes 786440 | tf_op jit(solution)/shard_map/ppermute | solution.py:952
  130.9 15.2 %collective-permute-start.18 = (bf16[256,512]{1,0:T(8,128)(2,1)S(1)}, bf16[256,512]{1,0:T(8,128)(2,1)S(1)}, u32[]{:S(2)}, u32[]{:S(2)}) collective-permute-start(bf16[256,512]{1,0:T(8,128)(2,1)S(1)} %get-tuple-element.270), channel_id=1, source_target_pairs={{0,24},{8,16},{16,8},{24,0},{1,25},{9,17},{17,9},{25,1},{2,26},{10... | collective-permute-start | bytes 786440 | tf_op jit(solution)/shard_map/ppermute | solution.py:952
  149.9 22.9 %collective-permute-start.19 = (bf16[384,512]{1,0:T(8,128)(2,1)S(1)}, bf16[384,512]{1,0:T(8,128)(2,1)S(1)}, u32[]{:S(2)}, u32[]{:S(2)}) collective-permute-start(bf16[384,512]{1,0:T(8,128)(2,1)S(1)} %get-tuple-element.292), channel_id=1, source_target_pairs={{0,8},{8,0},{16,24},{24,16},{1,9},{9,1},{17,25},{25,17},{2,10},{10... | collective-permute-start | bytes 1179656 | tf_op jit(solution)/shard_map/ppermute | solution.py:952
  151.9 20.9 %collective-permute-start.20 = (bf16[384,512]{1,0:T(8,128)(2,1)S(1)}, bf16[384,512]{1,0:T(8,128)(2,1)S(1)}, u32[]{:S(2)}, u32[]{:S(2)}) collective-permute-start(bf16[384,512]{1,0:T(8,128)(2,1)S(1)} %get-tuple-element.293), channel_id=1, source_target_pairs={{0,16},{8,24},{16,0},{24,8},{1,17},{9,25},{17,1},{25,9},{2,18},{10... | collective-permute-start | bytes 1179656 | tf_op jit(solution)/shard_map/ppermute | solution.py:952
  151.9 20.9 %collective-permute-start.21 = (bf16[384,512]{1,0:T(8,128)(2,1)S(1)}, bf16[384,512]{1,0:T(8,128)(2,1)S(1)}, u32[]{:S(2)}, u32[]{:S(2)}) collective-permute-start(bf16[384,512]{1,0:T(8,128)(2,1)S(1)} %get-tuple-element.294), channel_id=1, source_target_pairs={{0,24},{8,16},{16,8},{24,0},{1,25},{9,17},{17,9},{25,1},{2,26},{10... | collective-permute-start | bytes 1179656 | tf_op jit(solution)/shard_map/ppermute | solution.py:952
  153.5 23.2 %copy-start.5 = (bf16[256,512]{1,0:T(8,128)(2,1)S(1)}, bf16[256,512]{1,0:T(8,128)(2,1)}, u32[]{:S(2)}) copy-start(bf16[256,512]{1,0:T(8,128)(2,1)} %get-tuple-element.303.refs_2_) | copy-start | bytes 786436
  153.5 23.2 %copy-start.6 = (bf16[256,512]{1,0:T(8,128)(2,1)S(1)}, bf16[256,512]{1,0:T(8,128)(2,1)}, u32[]{:S(2)}) copy-start(bf16[256,512]{1,0:T(8,128)(2,1)} %get-tuple-element.304.refs_3_) | copy-start | bytes 786436
  153.5 23.2 %copy-start.13 = (s32[10]{0:T(128)S(1)}, s32[10]{0:T(128)}, u32[]{:S(2)}) copy-start(s32[10]{0:T(128)} %stack.81.place_ref) | copy-start | bytes 124
  172.8 6.6 %copy-start.1 = (bf16[4,4,64,512]{3,2,1,0:T(8,128)(2,1)S(1)}, bf16[4,4,64,512]{3,2,1,0:T(8,128)(2,1)}, u32[]{:S(2)}) copy-start(bf16[4,4,64,512]{3,2,1,0:T(8,128)(2,1)} %get-tuple-element.295.refs_0_) | copy-start | bytes 3145732
  172.9 6.5 %collective-permute-start.22 = (bf16[4,4,64,512]{3,2,1,0:T(8,128)(2,1)}, bf16[4,4,64,512]{3,2,1,0:T(8,128)(2,1)S(1)}, u32[]{:S(2)}, u32[]{:S(2)}) collective-permute-start(bf16[4,4,64,512]{3,2,1,0:T(8,128)(2,1)} %get-tuple-element.296), channel_id=1, source_target_pairs={{0,1},{1,0},{2,3},{3,2},{4,5},{5,4},{6,7},{7,6},{8,9},{9,8},{10,11... | collective-permute-start | bytes 3145736 | tf_op jit(solution)/shard_map/ppermute | solution.py:933
  173.0 3.7 %collective-permute-start.23 = (bf16[512,512]{1,0:T(8,128)(2,1)}, bf16[512,512]{1,0:T(8,128)(2,1)S(1)}, u32[]{:S(2)}, u32[]{:S(2)}) collective-permute-start(bf16[512,512]{1,0:T(8,128)(2,1)} %get-tuple-element.305), channel_id=1, source_target_pairs={{0,1},{1,0},{2,3},{3,2},{4,5},{5,4},{6,7},{7,6},{8,9},{9,8},{10,11... | collective-permute-start | bytes 1572872 | tf_op jit(solution)/shard_map/ppermute | solution.py:933
  180.2 9.2 %collective-permute-start.24 = (bf16[256,512]{1,0:T(8,128)(2,1)S(1)}, bf16[256,512]{1,0:T(8,128)(2,1)S(1)}, u32[]{:S(2)}, u32[]{:S(2)}) collective-permute-start(bf16[256,512]{1,0:T(8,128)(2,1)S(1)} %get-tuple-element.310), channel_id=1, source_target_pairs={{0,8},{8,0},{16,24},{24,16},{1,9},{9,1},{17,25},{25,17},{2,10},{10... | collective-permute-start | bytes 786440 | tf_op jit(solution)/shard_map/ppermute | solution.py:952
  182.2 14.2 %collective-permute-start.25 = (bf16[256,512]{1,0:T(8,128)(2,1)S(1)}, bf16[256,512]{1,0:T(8,128)(2,1)S(1)}, u32[]{:S(2)}, u32[]{:S(2)}) collective-permute-start(bf16[256,512]{1,0:T(8,128)(2,1)S(1)} %get-tuple-element.311), channel_id=1, source_target_pairs={{0,16},{8,24},{16,0},{24,8},{1,17},{9,25},{17,1},{25,9},{2,18},{10... | collective-permute-start | bytes 786440 | tf_op jit(solution)/shard_map/ppermute | solution.py:952
  182.5 13.9 %collective-permute-start.26 = (bf16[256,512]{1,0:T(8,128)(2,1)S(1)}, bf16[256,512]{1,0:T(8,128)(2,1)S(1)}, u32[]{:S(2)}, u32[]{:S(2)}) collective-permute-start(bf16[256,512]{1,0:T(8,128)(2,1)S(1)} %get-tuple-element.312), channel_id=1, source_target_pairs={{0,24},{8,16},{16,8},{24,0},{1,25},{9,17},{17,9},{25,1},{2,26},{10... | collective-permute-start | bytes 786440 | tf_op jit(solution)/shard_map/ppermute | solution.py:952
  184.6 34.2 %copy-start.15 = (bf16[2,256,512]{2,1,0:T(8,128)(2,1)S(1)}, bf16[2,256,512]{2,1,0:T(8,128)(2,1)}, u32[]{:S(2)}) copy-start(bf16[2,256,512]{2,1,0:T(8,128)(2,1)} %copy-done.14) | copy-start | bytes 1572868
  184.6 34.2 %copy-start.17 = (bf16[2,256,512]{2,1,0:T(8,128)(2,1)S(1)}, bf16[2,256,512]{2,1,0:T(8,128)(2,1)}, u32[]{:S(2)}) copy-start(bf16[2,256,512]{2,1,0:T(8,128)(2,1)} %copy-done.16) | copy-start | bytes 1572868
  184.6 35.4 %collective-permute-start.33 = (bf16[2,256,512]{2,1,0:T(8,128)(2,1)S(1)}, bf16[2,256,512]{2,1,0:T(8,128)(2,1)S(1)}, u32[]{:S(2)}, u32[]{:S(2)}) collective-permute-start(bf16[2,256,512]{2,1,0:T(8,128)(2,1)S(1)} %get-tuple-element.334), channel_id=1, source_target_pairs={{0,0},{1,8},{2,2},{3,10},{4,4},{5,12},{6,6},{7,14},{8,1},{9,9},{10... | collective-permute-start | bytes 1572872 | tf_op jit(solution)/shard_map/ppermute | solution.py:924
  185.4 34.5 %collective-permute-start.34 = (bf16[2,256,512]{2,1,0:T(8,128)(2,1)S(1)}, bf16[2,256,512]{2,1,0:T(8,128)(2,1)}, u32[]{:S(2)}, u32[]{:S(2)}) collective-permute-start(bf16[2,256,512]{2,1,0:T(8,128)(2,1)S(1)} %get-tuple-element.335), channel_id=1, source_target_pairs={{0,24},{1,16},{2,26},{3,18},{4,28},{5,20},{6,30},{7,22},{8,25},{9,... | collective-permute-start | bytes 1572872 | tf_op jit(solution)/shard_map/ppermute | solution.py:924
  197.1 11.2 %collective-permute-start.27 = (bf16[192,512]{1,0:T(8,128)(2,1)S(1)}, bf16[192,512]{1,0:T(8,128)(2,1)}, u32[]{:S(2)}, u32[]{:S(2)}) collective-permute-start(bf16[192,512]{1,0:T(8,128)(2,1)S(1)} %get-tuple-element.326), channel_id=1, source_target_pairs={{0,2},{1,3},{2,0},{3,1},{4,6},{5,7},{6,4},{7,5},{8,10},{9,11},{10,... | collective-permute-start | bytes 589832 | tf_op jit(solution)/shard_map/ppermute | solution.py:960
  198.5 17.3 %collective-permute-start.28 = (bf16[192,512]{1,0:T(8,128)(2,1)S(1)}, bf16[192,512]{1,0:T(8,128)(2,1)}, u32[]{:S(2)}, u32[]{:S(2)}) collective-permute-start(bf16[192,512]{1,0:T(8,128)(2,1)S(1)} %get-tuple-element.327), channel_id=1, source_target_pairs={{0,4},{1,5},{2,6},{3,7},{4,0},{5,1},{6,2},{7,3},{8,12},{9,13},{10,... | collective-permute-start | bytes 589832 | tf_op jit(solution)/shard_map/ppermute | solution.py:960
  201.2 15.7 %collective-permute-start.29 = (bf16[192,512]{1,0:T(8,128)(2,1)S(1)}, bf16[192,512]{1,0:T(8,128)(2,1)}, u32[]{:S(2)}, u32[]{:S(2)}) collective-permute-start(bf16[192,512]{1,0:T(8,128)(2,1)S(1)} %get-tuple-element.328), channel_id=1, source_target_pairs={{0,6},{1,7},{2,4},{3,5},{4,2},{5,3},{6,0},{7,1},{8,14},{9,15},{10,... | collective-permute-start | bytes 589832 | tf_op jit(solution)/shard_map/ppermute | solution.py:960
  208.3 11.7 %collective-permute-start.30 = (bf16[272,512]{1,0:T(8,128)(2,1)S(1)}, bf16[272,512]{1,0:T(8,128)(2,1)S(1)}, u32[]{:S(2)}, u32[]{:S(2)}) collective-permute-start(bf16[272,512]{1,0:T(8,128)(2,1)S(1)} %get-tuple-element.331), channel_id=1, source_target_pairs={{0,8},{8,0},{16,24},{24,16},{1,9},{9,1},{17,25},{25,17},{2,10},{10... | collective-permute-start | bytes 835592 | tf_op jit(solution)/shard_map/ppermute | solution.py:952
  215.8 15.2 %collective-permute-start.31 = (bf16[272,512]{1,0:T(8,128)(2,1)S(1)}, bf16[272,512]{1,0:T(8,128)(2,1)S(1)}, u32[]{:S(2)}, u32[]{:S(2)}) collective-permute-start(bf16[272,512]{1,0:T(8,128)(2,1)S(1)} %get-tuple-element.332), channel_id=1, source_target_pairs={{0,16},{8,24},{16,0},{24,8},{1,17},{9,25},{17,1},{25,9},{2,18},{10... | collective-permute-start | bytes 835592 | tf_op jit(solution)/shard_map/ppermute | solution.py:952
  216.8 14.2 %collective-permute-start.32 = (bf16[272,512]{1,0:T(8,128)(2,1)S(1)}, bf16[272,512]{1,0:T(8,128)(2,1)S(1)}, u32[]{:S(2)}, u32[]{:S(2)}) collective-permute-start(bf16[272,512]{1,0:T(8,128)(2,1)S(1)} %get-tuple-element.333), channel_id=1, source_target_pairs={{0,24},{8,16},{16,8},{24,0},{1,25},{9,17},{17,9},{25,1},{2,26},{10... | collective-permute-start | bytes 835592 | tf_op jit(solution)/shard_map/ppermute | solution.py:952
  232.3 8.4 %collective-permute-start.37 = (bf16[336,512]{1,0:T(8,128)(2,1)S(1)}, bf16[336,512]{1,0:T(8,128)(2,1)S(1)}, u32[]{:S(2)}, u32[]{:S(2)}) collective-permute-start(bf16[336,512]{1,0:T(8,128)(2,1)S(1)} %pad_maximum_fusion.2.refs_0_), channel_id=1, source_target_pairs={{0,24},{8,16},{16,8},{24,0},{1,25},{9,17},{17,9},{25,1},{2,26},{10... | collective-permute-start | bytes 1032200 | tf_op jit(solution)/shard_map/ppermute | solution.py:952
  235.4 8.9 %collective-permute-start.36 = (bf16[336,512]{1,0:T(8,128)(2,1)S(1)}, bf16[336,512]{1,0:T(8,128)(2,1)S(1)}, u32[]{:S(2)}, u32[]{:S(2)}) collective-permute-start(bf16[336,512]{1,0:T(8,128)(2,1)S(1)} %pad_maximum_fusion.2.refs_0_), channel_id=1, source_target_pairs={{0,16},{8,24},{16,0},{24,8},{1,17},{9,25},{17,1},{25,9},{2,18},{10... | collective-permute-start | bytes 1032200 | tf_op jit(solution)/shard_map/ppermute | solution.py:952
  235.7 8.6 %collective-permute-start.35 = (bf16[336,512]{1,0:T(8,128)(2,1)S(1)}, bf16[336,512]{1,0:T(8,128)(2,1)S(1)}, u32[]{:S(2)}, u32[]{:S(2)}) collective-permute-start(bf16[336,512]{1,0:T(8,128)(2,1)S(1)} %pad_maximum_fusion.2.refs_0_), channel_id=1, source_target_pairs={{0,8},{8,0},{16,24},{24,16},{1,9},{9,1},{17,25},{25,17},{2,10},{10... | collective-permute-start | bytes 1032200 | tf_op jit(solution)/shard_map/ppermute | solution.py:952
  (23 other events, 43.4 us)
Sparse Core Ops, SparseCore 0:
  84.5 50.7 reduce-scatter.2
  147.0 56.6 reduce-scatter.4
where the time goes:
time: 259 us; the launch traced here: 256 us
  Pallas kernels  137 us (53%)
  starting transfers between devices  44.2 us (17%)
  waiting for transfers between devices  40 us (15%)
  between operations  14.8 us (6%)
  local copies, waits for them, and re-layouts  13.1 us (5%)
  other arithmetic  7.23 us (3%)
    pallas_call x8, Pallas kernels, run(): pl.pallas_call(body, out_shape=shapes, in_specs=[pl.BlockSpec(memory_spac...  132 us
    ppermute x15, waiting for transfers between devices, to_quarters(): lax.ppermute(part, 'pipe', [(i, i ^ step) for i in range(quarters)])  24 us
    ppermute x15, starting transfers between devices, to_quarters(): lax.ppermute(part, 'pipe', [(i, i ^ step) for i in range(quarters)])  19 us
    unnamed x62, local copies, waits for them, and re-layouts  9.08 us
    ppermute x3, waiting for transfers between devices, to_planes(): lax.ppermute(part, 'dp', [(i, i ^ 2 * step) for i in range(groups)])  8.92 us
    ppermute x12, starting transfers between devices, to_other_core(): return lax.ppermute(value, 'dp', self.cores)  8.4 us
    ppermute x4, starting transfers between devices, to_work(): lax.ppermute(part, ('pipe', 'dp'), pairs)  7.24 us
    pallas_call x7, Pallas kernels, small_kernel(): pl.pallas_call(body, out_shape=outs, in_specs=[pl.BlockSpec(memory_space=...  5.25 us
  transfers between devices with their start and end apart: 40, of which 11 were waited for; matrix products, arithmetic and copies ran while one was open for 4% of the time, Pallas kernels for 38%

commit v1 on v0

--- a/solution.py
+++ b/solution.py
@@ -534,7 +534,7 @@
 
 
 def put_norm(io, normed, inverse, normed_ref, inverse_ref):
-    normed_ref[...] = normed
+    normed_ref[...] = normed.astype(normed_ref.dtype)
     inverse_ref[...] = jnp.broadcast_to(inverse, inverse_ref.shape)
     io.send(normed_ref, inverse_ref)
 
@@ -582,7 +582,7 @@
     put_norm(io, normed, inverse, io.n, io.i)
     spread = spread_of(io, io.grads)
     fill_bias(io.place, io.place[4], False, bias_ref)
-    first = io.n[...] * io.gain[...] + io.offset[...]
+    first = normed * io.gain[...] + io.offset[...]
     first_low = first.astype(BF)
     io.first[...] = first_low
     io.send(io.first)
@@ -606,7 +606,7 @@
         io.result[2 * half + 1] = output[rows]
     io.send(io.result)
     back, dscale, dcenter = norm_backward(io.cotangent[...].astype(F32), n3, i3, io.scale[...])
-    io.dr[...] = back
+    io.dr[...] = back.astype(BF)
     io.send(io.dr)
     w1, w2 = io.w1, io.w2
 
@@ -639,7 +639,7 @@
     io.dmem_other[...] = dc_other.astype(BF)
     io.dmem_own[...] = dc_own.astype(BF)
     io.send(io.dmem_other, io.dmem_own)
-    dv1, dgain, doffset = norm_backward(dv2 + du, io.n[...], io.i[:, :1], io.gain[...])
+    dv1, dgain, doffset = norm_backward(dv2 + du, io.n[...].astype(F32), io.i[:, :1], io.gain[...])
     io.dv1[...] = dv1
     io.send(io.dv1)
     put_rows(io.vecs, 0, (dgain, doffset))
@@ -653,7 +653,7 @@
     )
     io.dc_other[...] = dc_other.astype(BF)
     io.send(io.dc_other)
-    io.du[...] = (dv + io.extra[...] + du + dc_own).astype(BF)
+    io.du[...] = (dv + io.extra[...].astype(F32) + du + dc_own).astype(BF)
     io.send(io.du)
 
 
@@ -710,8 +710,8 @@
     spread = spread_of(io, io.grads)
     dmemory = (io.dmem_own[...].astype(F32) + io.dmem_came[...].astype(F32)).astype(BF).astype(F32)
     total = io.cotangent[...].astype(F32) + dmemory
-    back, dscale, dcenter = norm_backward(total, io.n1[...], io.i1[:, :1], io.scale[...])
-    io.dr[...] = back
+    back, dscale, dcenter = norm_backward(total, io.n1[...].astype(F32), io.i1[:, :1], io.scale[...])
+    io.dr[...] = back.astype(BF)
     io.send(io.dr)
 
     def parts(number):
@@ -726,7 +726,7 @@
     vecs = io.vecs
     dhidden, dshift = ffn_backward(io, spread, back, io.hidden[...], parts, vecs.at[0:4])
     dlow = (back + dhidden).astype(BF).astype(F32)
-    dv0, dgain, doffset = norm_backward(dlow, io.n0[...], io.i0[:, :1], io.gain[...])
+    dv0, dgain, doffset = norm_backward(dlow, io.n0[...].astype(F32), io.i0[:, :1], io.gain[...])
     io.dv[...] = dv0
     io.send(io.dv)
     top, cross = io.top_vecs, io.cross_vecs
@@ -1049,8 +1049,8 @@
              w2=source_contract),
         dict(gain=row(source_gain), offset=row(source_offset), b1=row(source_bias), b2=row(source_shift),
              scale=row(source_scale), center=row(source_center)),
-        dict(**saved, n0=sheet, i0=lanes, hidden=shape(rows, width), active=shape(rows, wide),
-             slope=shape(rows, wide), n1=sheet, i1=lanes, memory=shape(rows, width)),
+        dict(**saved, n0=shape(rows, width), i0=lanes, hidden=shape(rows, width), active=shape(rows, wide),
+             slope=shape(rows, wide), n1=shape(rows, width), i1=lanes, memory=shape(rows, width)),
         [flat_bias],
     )
     *late, memory = gate(*late, encoder.memory)
@@ -1065,8 +1065,8 @@
         dict(gain=row(target_gain), offset=row(target_offset), cross_gain=row(cross_gain),
              cross_offset=row(cross_offset), b1=row(target_bias), b2=row(target_shift), scale=row(target_scale),
              center=row(target_center)),
-        dict(sq=saved.q, sk=saved.k, sv=saved.v, sot=saved.ot, slse=saved.lse, n=sheet, i=lanes, **saved,
-             first=shape(rows, width), result=Ends([shape(2, block, width)] * 2), dr=sheet, dv=sheet,
+        dict(sq=saved.q, sk=saved.k, sv=saved.v, sot=saved.ot, slse=saved.lse, n=shape(rows, width), i=lanes, **saved,
+             first=shape(rows, width), result=Ends([shape(2, block, width)] * 2), dr=shape(rows, width), dv=sheet,
              vecs=shape(16, width, dtype=F32), grads=top_grads),
         [causal_bias, flat_bias, pltpu.VMEM((rows, wide), BF), pltpu.VMEM((rows, wide), BF)],
     )
@@ -1114,7 +1114,7 @@
              w1=Blocks(source_expand, 1), active=Blocks(encoder.active, 1), hidden=encoder.hidden, n0=encoder.n0,
              i0=encoder.i0),
         dict(scale=row(source_scale), gain=row(source_gain), top_vecs=top.vecs, cross_vecs=cross.vecs),
-        dict(dr=sheet, dv=sheet, vecs=shape(vec_rows, width, dtype=F32), grads=source_ffn_grads),
+        dict(dr=shape(rows, width), dv=sheet, vecs=shape(vec_rows, width, dtype=F32), grads=source_ffn_grads),
     )
     source_ffn, dtarget_came, target_came, early = after(source_ffn, dtarget_came, target_came, early)
     dv0, middle = source_ffn.dv, ()

time: 259 us -> 259 us (level)
  no operation moved by 1% of the time
where the time goes in v1:
time: 259 us; the launch traced here: 256 us
  Pallas kernels  137 us (53%)
  starting transfers between devices  44.3 us (17%)
  waiting for transfers between devices  39.9 us (15%)
  between operations  14.8 us (6%)
  local copies, waits for them, and re-layouts  13.1 us (5%)
  other arithmetic  7.23 us (3%)
    pallas_call x8, Pallas kernels, run(): pl.pallas_call(body, out_shape=shapes, in_specs=[pl.BlockSpec(memory_spac...  132 us
    ppermute x15, waiting for transfers between devices, to_quarters(): lax.ppermute(part, 'pipe', [(i, i ^ step) for i in range(quarters)])  23.9 us
    ppermute x15, starting transfers between devices, to_quarters(): lax.ppermute(part, 'pipe', [(i, i ^ step) for i in range(quarters)])  19.1 us
    ppermute x3, waiting for transfers between devices, to_planes(): lax.ppermute(part, 'dp', [(i, i ^ 2 * step) for i in range(groups)])  9.08 us
    unnamed x62, local copies, waits for them, and re-layouts  9.06 us
    ppermute x12, starting transfers between devices, to_other_core(): return lax.ppermute(value, 'dp', self.cores)  8.38 us
    ppermute x4, starting transfers between devices, to_work(): lax.ppermute(part, ('pipe', 'dp'), pairs)  7.24 us
    pallas_call x7, Pallas kernels, small_kernel(): pl.pallas_call(body, out_shape=outs, in_specs=[pl.BlockSpec(memory_space=...  5.25 us
  transfers between devices with their start and end apart: 40, of which 11 were waited for; matrix products, arithmetic and copies ran while one was open for 4% of the time, Pallas kernels for 38%

profile of v1, /device:TPU:0, one launch (start us, length us, event | category | flops | bytes accessed | tf_op | source)
XLA Modules:
  0.0 256.1 jit_solution(13034634447539289801)
XLA Ops:
  8.4 1.1 select_bitcast_fusion.6
  9.5 3.5 %collective-permute-start.1 = (bf16[256,512]{1,0:T(8,128)(2,1)S(1)}, bf16[256,512]{1,0:T(8,128)(2,1)S(1)}, u32[]{:S(2)}, u32[]{:S(2)}) collective-permute-start(bf16[256,512]{1,0:T(8,128)(2,1)S(1)} %get-tuple-element.383), channel_id=1, source_target_pairs={{0,24},{1,16},{2,26},{3,18},{4,28},{5,20},{6,30},{7,22},{8,25},{9,... | collective-permute-start | bytes 786440 | tf_op jit(solution)/shard_map/ppermute | solution.py:918
  13.0 1.4 collective-permute-start
  14.3 1.5 pad_maximum_fusion
  17.2 1.9 stack.81.place_ref
  19.1 1.4 collective-permute-start.5
  21.3 1.7 collective-permute-start.4
  23.7 20.1 %encoder.1 = (bf16[512,512]{1,0:T(8,128)(2,1)}, bf16[1024,512]{1,0:T(8,128)(2,1)}, bf16[1024,512]{1,0:T(8,128)(2,1)}, f32[512,512]{1,0:T(8,128)}, f32[8,512]{1,0...) custom-call(s32[10]{0:T(128)} %stack.81.place_ref, ...), custom_call_target="tpu_custom_call" | custom-call | flops 8589934592 | bytes 17842176 | tf_op jit(solution)/shard_map/encoder/pallas_call | solution.py:511
  43.8 2.1 collective-permute-start.9
  46.5 1.3 collective-permute-done.8.refs_12_.refs_10_
  49.1 35.0 %decoder.1 = (bf16[512,512]{1,0:T(8,128)(2,1)}, bf16[1024,512]{1,0:T(8,128)(2,1)}, bf16[1024,512]{1,0:T(8,128)(2,1)}, f32[512,512]{1,0:T(8,128)}, f32[8,512]{1,0...) custom-call(s32[10]{0:T(128)} %stack.81.place_ref, ...), custom_call_target="tpu_custom_call" | custom-call | flops 19327352832 | bytes 28639232 | tf_op jit(solution)/shard_map/decoder/pallas_call | solution.py:511
  84.2 0.9 copy-done.25
  86.1 1.5 collective-permute-start.11
  87.6 20.2 %cross_back.1 = (bf16[512,512]{1,0:T(8,128)(2,1)}, bf16[512,512]{1,0:T(8,128)(2,1)}, f32[512,512]{1,0:T(8,128)}, f32[8,512]{1,0:T(8,128)}, bf16[4,4,64,512]{3,2,...) custom-call(s32[10]{0:T(128)} %stack.81.place_ref, f32[1,512]{1,0:T(1,128)} %bitcast.80, ...), custom_call_target="tpu_custom_call" | custom-call | flops 15032385536 | bytes 13402112 | tf_op jit(solution)/shard_map/cross_back/pallas_call | solution.py:511
  107.9 2.3 collective-permute-start.12
  110.3 16.6 %target_back.1 = (bf16[512,512]{1,0:T(8,128)(2,1)}, bf16[256,512]{1,0:T(8,128)(2,1)}, bf16[256,512]{1,0:T(8,128)(2,1)}, bf16[4,4,64,512]{3,2,1,0:T(8,128)(2,1)}, bf16[4,4,64,512]{3,2,1,0:T(8,128)(2,1)}) custom-call(s32[10]{0:T(128)} %stack.81.place_ref, f32[512,512]{1,0:T(8,128)} %get-tuple-element.234.refs_0_, bf16[512,512]{1,0:T(8,128)(2,1)} %refs_1_.2, ...), custom_call_target="tpu_custom_call" | custom-call | flops 15032385536 | bytes 12599296 | tf_op jit(solution)/shard_map/target_back/pallas_call | solution.py:511
  128.5 2.2 collective-permute-start.16
  130.7 1.5 collective-permute-start.18
  132.3 13.6 %source_ffn.1 = (bf16[512,512]{1,0:T(8,128)(2,1)}, f32[512,512]{1,0:T(8,128)}, f32[64,512]{1,0:T(8,128)}, bf16[8,4,144,512]{3,2,1,0:T(8,128)(2,1)}) custom-call(s32[10]{0:T(128)} %stack.81.place_ref, f32[1,512]{1,0:T(1,128)} %bitcast.84, f32[1,512]{1,0:T(1,128)} %bitcast.82, f32[16,512]{1,0:T(8,128)} %get-tuple-element.230.refs_2_, ...), custom_call_target="tpu_custom_call" | custom-call | flops 4294967296 | bytes 19529728 | tf_op jit(solution)/shard_map/source_ffn/pallas_call | solution.py:511
  146.7 1.2 copy-done.2
  147.9 1.0 copy-done.4
  149.7 2.0 collective-permute-start.19
  151.7 1.5 collective-permute-start.21
  153.3 19.3 %source_back.1 = (bf16[512,512]{1,0:T(8,128)(2,1)}, bf16[256,512]{1,0:T(8,128)(2,1)}, bf16[256,512]{1,0:T(8,128)(2,1)}, bf16[4,4,64,512]{3,2,1,0:T(8,128)(2,1)}, bf16[4,4,64,512]{3,2,1,0:T(8,128)(2,1)}) custom-call(s32[10]{0:T(128)} %stack.81.place_ref, f32[512,512]{1,0:T(8,128)} %get-tuple-element.279.refs_0_, bf16[512,512]{1,0:T(8,128)(2,1)} %refs_1_.3, ...), custom_call_target="tpu_custom_call" | custom-call | flops 15032385536 | bytes 11550720 | tf_op jit(solution)/shard_map/source_back/pallas_call | solution.py:511
  173.3 3.2 %collective-permute-done.23.refs_4_ = bf16[512,512]{1,0:T(8,128)(2,1)S(1)} collective-permute-done((bf16[512,512]{1,0:T(8,128)(2,1)}, bf16[512,512]{1,0:T(8,128)(2,1)S(1)}, u32[]{:S(2)}, u32[]{:S(2)}) %collective-permute-start.23) | collective-permute-done | bytes 524320 | tf_op jit(solution)/shard_map/ppermute | solution.py:933
  180.0 2.0 collective-permute-start.24
  182.3 1.3 collective-permute-start.26
  185.2 1.7 collective-permute-start.34
  187.0 2.2 collective-permute-done.24.refs_1_
  189.2 7.1 %collective-permute-done.25.refs_2_ = bf16[256,512]{1,0:T(8,128)(2,1)S(1)} collective-permute-done((bf16[256,512]{1,0:T(8,128)(2,1)S(1)}, bf16[256,512]{1,0:T(8,128)(2,1)S(1)}, u32[]{:S(2)}, u32[]{:S(2)}) %collective-permute-start.25) | collective-permute-done | bytes 262176 | tf_op jit(solution)/shard_map/ppermute | solution.py:952
  197.0 1.3 collective-permute-start.27
  198.3 2.7 %collective-permute-start.28 = (bf16[192,512]{1,0:T(8,128)(2,1)S(1)}, bf16[192,512]{1,0:T(8,128)(2,1)}, u32[]{:S(2)}, u32[]{:S(2)}) collective-permute-start(bf16[192,512]{1,0:T(8,128)(2,1)S(1)} %get-tuple-element.327), channel_id=1, source_target_pairs={{0,4},{1,5},{2,6},{3,7},{4,0},{5,1},{6,2},{7,3},{8,12},{9,13},{10,... | collective-permute-start | bytes 589832 | tf_op jit(solution)/shard_map/ppermute | solution.py:960
  201.5 2.0 reduce-scatter.5.cloned.1.call-done
  203.4 1.1 copy-done.3
  205.1 2.9 %collective-permute-done.27 = bf16[192,512]{1,0:T(8,128)(2,1)} collective-permute-done((bf16[192,512]{1,0:T(8,128)(2,1)S(1)}, bf16[192,512]{1,0:T(8,128)(2,1)}, u32[]{:S(2)}, u32[]{:S(2)}) %collective-permute-start.27) | collective-permute-done | bytes 196640 | tf_op jit(solution)/shard_map/ppermute | solution.py:960
  208.1 1.3 collective-permute-start.30
  209.4 6.1 %collective-permute-done.28 = bf16[192,512]{1,0:T(8,128)(2,1)} collective-permute-done((bf16[192,512]{1,0:T(8,128)(2,1)S(1)}, bf16[192,512]{1,0:T(8,128)(2,1)}, u32[]{:S(2)}, u32[]{:S(2)}) %collective-permute-start.28) | collective-permute-done | bytes 196640 | tf_op jit(solution)/shard_map/ppermute | solution.py:960
  215.5 1.1 collective-permute-start.31
  216.6 2.1 collective-permute-start.32
  218.8 1.1 fusion.2
  219.9 10.9 %collective-permute-done.31.refs_2_ = bf16[272,512]{1,0:T(8,128)(2,1)S(1)} collective-permute-done((bf16[272,512]{1,0:T(8,128)(2,1)S(1)}, bf16[272,512]{1,0:T(8,128)(2,1)S(1)}, u32[]{:S(2)}, u32[]{:S(2)}) %collective-permute-start.31) | collective-permute-done | bytes 278560 | tf_op jit(solution)/shard_map/ppermute | solution.py:952
  230.9 1.2 add_convert_fusion
  232.1 3.1 %collective-permute-start.37 = (bf16[336,512]{1,0:T(8,128)(2,1)S(1)}, bf16[336,512]{1,0:T(8,128)(2,1)S(1)}, u32[]{:S(2)}, u32[]{:S(2)}) collective-permute-start(bf16[336,512]{1,0:T(8,128)(2,1)S(1)} %pad_maximum_fusion.2.refs_0_), channel_id=1, source_target_pairs={{0,24},{8,16},{16,8},{24,0},{1,25},{9,17},{17,9},{25,1},{2,26},{10... | collective-permute-start | bytes 1032200 | tf_op jit(solution)/shard_map/ppermute | solution.py:952
  235.8 1.2 select_bitcast_fusion.3
  237.2 1.8 unpack_first.1
  239.0 1.5 slice_bitcast_fusion
  240.5 3.6 %collective-permute-done.36.refs_2_ = bf16[336,512]{1,0:T(8,128)(2,1)S(1)} collective-permute-done((bf16[336,512]{1,0:T(8,128)(2,1)S(1)}, bf16[336,512]{1,0:T(8,128)(2,1)S(1)}, u32[]{:S(2)}, u32[]{:S(2)}) %collective-permute-start.36) | collective-permute-done | bytes 344096 | tf_op jit(solution)/shard_map/ppermute | solution.py:952
  244.1 5.0 %unpack_last.1 = (f32[64,512]{1,0:T(8,128)}, f32[64,1024]{1,0:T(8,128)}, f32[64,512]{1,0:T(8,128)}, f32[64,512]{1,0:T(8,128)}, f32[64,1024]{1,0:T(8,128)}, /*ind...) custom-call(s32[10]{0:T(128)S(1)} %copy-done.13, ...), custom_call_target="tpu_custom_call" | custom-call | bytes 2757632 | tf_op jit(solution)/shard_map/unpack_last/pallas_call | solution.py:511
  (130 shorter events, 18.9 us)
Async XLA Ops:
  7.2 139.5 %reduce-scatter.3.cloned.1.call-start = ((), (), s32[]{:S(2)}) async-start(), calls=%async_computation.2 | async-start | bytes 4718592 | tf_op jit(solution)/shard_map/reduce_scatter | solution.py:1075
  7.9 8.1 %collective-permute-start.2 = (s32[2,2]{1,0:T(2,128)S(1)}, s32[2,2]{1,0:T(2,128)S(1)}, u32[]{:S(2)}, u32[]{:S(2)}) collective-permute-start(s32[2,2]{1,0:T(2,128)S(1)} %pad_add_fusion), channel_id=1, source_target_pairs={{0,1},{1,0},{2,3},{3,2},{4,5},{5,4},{6,7},{7,6},{8,9},{9,8},{10,11... | collective-permute-start | bytes 56 | tf_op jit(solution)/shard_map/ppermute | solution.py:933
  9.5 9.6 %collective-permute-start.1 = (bf16[256,512]{1,0:T(8,128)(2,1)S(1)}, bf16[256,512]{1,0:T(8,128)(2,1)S(1)}, u32[]{:S(2)}, u32[]{:S(2)}) collective-permute-start(bf16[256,512]{1,0:T(8,128)(2,1)S(1)} %get-tuple-element.383), channel_id=1, source_target_pairs={{0,24},{1,16},{2,26},{3,18},{4,28},{5,20},{6,30},{7,22},{8,25},{9,... | collective-permute-start | bytes 786440 | tf_op jit(solution)/shard_map/ppermute | solution.py:918
  13.0 6.1 %collective-permute-start = (bf16[256,512]{1,0:T(8,128)(2,1)S(1)}, bf16[256,512]{1,0:T(8,128)(2,1)}, u32[]{:S(2)}, u32[]{:S(2)}) collective-permute-start(bf16[256,512]{1,0:T(8,128)(2,1)S(1)} %get-tuple-element.384), channel_id=1, source_target_pairs={{0,0},{1,8},{2,2},{3,10},{4,4},{5,12},{6,6},{7,14},{8,1},{9,9},{10... | collective-permute-start | bytes 786440 | tf_op jit(solution)/shard_map/ppermute | solution.py:918
  19.1 3.9 %collective-permute-start.5 = (bf16[256,512]{1,0:T(8,128)(2,1)}, bf16[256,512]{1,0:T(8,128)(2,1)S(1)}, u32[]{:S(2)}, u32[]{:S(2)}) collective-permute-start(bf16[256,512]{1,0:T(8,128)(2,1)} %collective-permute-done.refs_6_.refs_7_), channel_id=1, source_target_pairs={{0,1},{1,0},{2,3},{3,2},{4,5},{5,4},{6,7},{7,6},{8,9},{9,8},{10,11... | collective-permute-start | bytes 786440 | tf_op jit(solution)/shard_map/ppermute | solution.py:933
  20.5 2.5 collective-permute-start.6
  20.6 23.2 %collective-permute-start.3 = (bf16[3,256,512]{2,1,0:T(8,128)(2,1)S(1)}, bf16[3,256,512]{2,1,0:T(8,128)(2,1)S(1)}, u32[]{:S(2)}, u32[]{:S(2)}) collective-permute-start(bf16[3,256,512]{2,1,0:T(8,128)(2,1)S(1)} %get-tuple-element.203), channel_id=1, source_target_pairs={{0,0},{1,8},{2,2},{3,10},{4,4},{5,12},{6,6},{7,14},{8,1},{9,9},{10... | collective-permute-start | bytes 2359304 | tf_op jit(solution)/shard_map/ppermute | solution.py:918
  21.3 22.6 %collective-permute-start.4 = (bf16[3,256,512]{2,1,0:T(8,128)(2,1)S(1)}, bf16[3,256,512]{2,1,0:T(8,128)(2,1)S(1)}, u32[]{:S(2)}, u32[]{:S(2)}) collective-permute-start(bf16[3,256,512]{2,1,0:T(8,128)(2,1)S(1)} %get-tuple-element.204), channel_id=1, source_target_pairs={{0,24},{1,16},{2,26},{3,18},{4,28},{5,20},{6,30},{7,22},{8,25},{9,... | collective-permute-start | bytes 2359304 | tf_op jit(solution)/shard_map/ppermute | solution.py:918
  43.8 4.3 %collective-permute-start.9 = (bf16[512,512]{1,0:T(8,128)(2,1)}, bf16[512,512]{1,0:T(8,128)(2,1)S(1)}, u32[]{:S(2)}, u32[]{:S(2)}) collective-permute-start(bf16[512,512]{1,0:T(8,128)(2,1)} %get-tuple-element.210.refs_16_.refs_9_), channel_id=1, source_target_pairs={{0,1},{1,0},{2,3},{3,2},{4,5},{5,4},{6,7},{7,6},{8,9},{9,8},{10,11... | collective-permute-start | bytes 1572872 | tf_op jit(solution)/shard_map/ppermute | solution.py:933
  46.0 1.9 collective-permute-start.8
  46.0 2.2 collective-permute-start.7
  84.2 119.3 %reduce-scatter.5.cloned.1.call-start = ((), (), s32[]{:S(2)}) async-start(), calls=%async_computation.3 | async-start | bytes 5308416 | tf_op jit(solution)/shard_map/reduce_scatter | solution.py:1122
  85.2 22.7 %collective-permute-start.10 = (bf16[2,256,512]{2,1,0:T(8,128)(2,1)S(1)}, bf16[2,256,512]{2,1,0:T(8,128)(2,1)S(1)}, u32[]{:S(2)}, u32[]{:S(2)}) collective-permute-start(bf16[2,256,512]{2,1,0:T(8,128)(2,1)S(1)} %copy-done.25), channel_id=1, source_target_pairs={{0,0},{1,8},{2,2},{3,10},{4,4},{5,12},{6,6},{7,14},{8,1},{9,9},{10... | collective-permute-start | bytes 1572872 | tf_op jit(solution)/shard_map/ppermute | solution.py:924
  86.1 21.8 %collective-permute-start.11 = (bf16[2,256,512]{2,1,0:T(8,128)(2,1)S(1)}, bf16[2,256,512]{2,1,0:T(8,128)(2,1)S(1)}, u32[]{:S(2)}, u32[]{:S(2)}) collective-permute-start(bf16[2,256,512]{2,1,0:T(8,128)(2,1)S(1)} %copy-done.24), channel_id=1, source_target_pairs={{0,24},{1,16},{2,26},{3,18},{4,28},{5,20},{6,30},{7,22},{8,25},{9,... | collective-permute-start | bytes 1572872 | tf_op jit(solution)/shard_map/ppermute | solution.py:924
  107.9 19.0 %collective-permute-start.12 = (bf16[512,512]{1,0:T(8,128)(2,1)}, bf16[512,512]{1,0:T(8,128)(2,1)S(1)}, u32[]{:S(2)}, u32[]{:S(2)}) collective-permute-start(bf16[512,512]{1,0:T(8,128)(2,1)} %get-tuple-element.246), channel_id=1, source_target_pairs={{0,1},{1,0},{2,3},{3,2},{4,5},{5,4},{6,7},{7,6},{8,9},{9,8},{10,11... | collective-permute-start | bytes 1572872 | tf_op jit(solution)/shard_map/ppermute | solution.py:933
  110.2 16.7 %collective-permute-start.13 = (bf16[4,4,64,512]{3,2,1,0:T(8,128)(2,1)}, bf16[4,4,64,512]{3,2,1,0:T(8,128)(2,1)S(1)}, u32[]{:S(2)}, u32[]{:S(2)}) collective-permute-start(bf16[4,4,64,512]{3,2,1,0:T(8,128)(2,1)} %get-tuple-element.247), channel_id=1, source_target_pairs={{0,1},{1,0},{2,3},{3,2},{4,5},{5,4},{6,7},{7,6},{8,9},{9,8},{10,11... | collective-permute-start | bytes 3145736 | tf_op jit(solution)/shard_map/ppermute | solution.py:933
  110.3 17.4 %copy-start = (bf16[4,4,64,512]{3,2,1,0:T(8,128)(2,1)S(1)}, bf16[4,4,64,512]{3,2,1,0:T(8,128)(2,1)}, u32[]{:S(2)}) copy-start(bf16[4,4,64,512]{3,2,1,0:T(8,128)(2,1)} %get-tuple-element.233.refs_0_) | copy-start | bytes 3145732
  110.3 17.4 %copy-start.11 = (s32[10]{0:T(128)S(1)}, s32[10]{0:T(128)}, u32[]{:S(2)}) copy-start(s32[10]{0:T(128)} %stack.81.place_ref) | copy-start | bytes 124
  126.9 19.7 %collective-permute-start.15 = (bf16[4,4,64,512]{3,2,1,0:T(8,128)(2,1)}, bf16[4,4,64,512]{3,2,1,0:T(8,128)(2,1)S(1)}, u32[]{:S(2)}, u32[]{:S(2)}) collective-permute-start(bf16[4,4,64,512]{3,2,1,0:T(8,128)(2,1)} %get-tuple-element.266), channel_id=1, source_target_pairs={{0,1},{1,0},{2,3},{3,2},{4,5},{5,4},{6,7},{7,6},{8,9},{9,8},{10,11... | collective-permute-start | bytes 3145736 | tf_op jit(solution)/shard_map/ppermute | solution.py:933
  127.6 19.0 %collective-permute-start.14 = (bf16[512,512]{1,0:T(8,128)(2,1)}, bf16[512,512]{1,0:T(8,128)(2,1)S(1)}, u32[]{:S(2)}, u32[]{:S(2)}) collective-permute-start(bf16[512,512]{1,0:T(8,128)(2,1)} %get-tuple-element.265), channel_id=1, source_target_pairs={{0,1},{1,0},{2,3},{3,2},{4,5},{5,4},{6,7},{7,6},{8,9},{9,8},{10,11... | collective-permute-start | bytes 1572872 | tf_op jit(solution)/shard_map/ppermute | solution.py:933
  128.5 17.4 %collective-permute-start.16 = (bf16[256,512]{1,0:T(8,128)(2,1)S(1)}, bf16[256,512]{1,0:T(8,128)(2,1)S(1)}, u32[]{:S(2)}, u32[]{:S(2)}) collective-permute-start(bf16[256,512]{1,0:T(8,128)(2,1)S(1)} %get-tuple-element.268), channel_id=1, source_target_pairs={{0,8},{8,0},{16,24},{24,16},{1,9},{9,1},{17,25},{25,17},{2,10},{10... | collective-permute-start | bytes 786440 | tf_op jit(solution)/shard_map/ppermute | solution.py:952
  130.7 15.2 %collective-permute-start.17 = (bf16[256,512]{1,0:T(8,128)(2,1)S(1)}, bf16[256,512]{1,0:T(8,128)(2,1)S(1)}, u32[]{:S(2)}, u32[]{:S(2)}) collective-permute-start(bf16[256,512]{1,0:T(8,128)(2,1)S(1)} %get-tuple-element.269), channel_id=1, source_target_pairs={{0,16},{8,24},{16,0},{24,8},{1,17},{9,25},{17,1},{25,9},{2,18},{10... | collective-permute-start | bytes 786440 | tf_op jit(solution)/shard_map/ppermute | solution.py:952
  130.7 15.2 %collective-permute-start.18 = (bf16[256,512]{1,0:T(8,128)(2,1)S(1)}, bf16[256,512]{1,0:T(8,128)(2,1)S(1)}, u32[]{:S(2)}, u32[]{:S(2)}) collective-permute-start(bf16[256,512]{1,0:T(8,128)(2,1)S(1)} %get-tuple-element.270), channel_id=1, source_target_pairs={{0,24},{8,16},{16,8},{24,0},{1,25},{9,17},{17,9},{25,1},{2,26},{10... | collective-permute-start | bytes 786440 | tf_op jit(solution)/shard_map/ppermute | solution.py:952
  149.7 22.9 %collective-permute-start.19 = (bf16[384,512]{1,0:T(8,128)(2,1)S(1)}, bf16[384,512]{1,0:T(8,128)(2,1)S(1)}, u32[]{:S(2)}, u32[]{:S(2)}) collective-permute-start(bf16[384,512]{1,0:T(8,128)(2,1)S(1)} %get-tuple-element.292), channel_id=1, source_target_pairs={{0,8},{8,0},{16,24},{24,16},{1,9},{9,1},{17,25},{25,17},{2,10},{10... | collective-permute-start | bytes 1179656 | tf_op jit(solution)/shard_map/ppermute | solution.py:952
  151.7 20.9 %collective-permute-start.20 = (bf16[384,512]{1,0:T(8,128)(2,1)S(1)}, bf16[384,512]{1,0:T(8,128)(2,1)S(1)}, u32[]{:S(2)}, u32[]{:S(2)}) collective-permute-start(bf16[384,512]{1,0:T(8,128)(2,1)S(1)} %get-tuple-element.293), channel_id=1, source_target_pairs={{0,16},{8,24},{16,0},{24,8},{1,17},{9,25},{17,1},{25,9},{2,18},{10... | collective-permute-start | bytes 1179656 | tf_op jit(solution)/shard_map/ppermute | solution.py:952
  151.7 20.9 %collective-permute-start.21 = (bf16[384,512]{1,0:T(8,128)(2,1)S(1)}, bf16[384,512]{1,0:T(8,128)(2,1)S(1)}, u32[]{:S(2)}, u32[]{:S(2)}) collective-permute-start(bf16[384,512]{1,0:T(8,128)(2,1)S(1)} %get-tuple-element.294), channel_id=1, source_target_pairs={{0,24},{8,16},{16,8},{24,0},{1,25},{9,17},{17,9},{25,1},{2,26},{10... | collective-permute-start | bytes 1179656 | tf_op jit(solution)/shard_map/ppermute | solution.py:952
  153.3 23.2 %copy-start.5 = (bf16[256,512]{1,0:T(8,128)(2,1)S(1)}, bf16[256,512]{1,0:T(8,128)(2,1)}, u32[]{:S(2)}) copy-start(bf16[256,512]{1,0:T(8,128)(2,1)} %get-tuple-element.303.refs_2_) | copy-start | bytes 786436
  153.3 23.2 %copy-start.6 = (bf16[256,512]{1,0:T(8,128)(2,1)S(1)}, bf16[256,512]{1,0:T(8,128)(2,1)}, u32[]{:S(2)}) copy-start(bf16[256,512]{1,0:T(8,128)(2,1)} %get-tuple-element.304.refs_3_) | copy-start | bytes 786436
  153.3 23.2 %copy-start.13 = (s32[10]{0:T(128)S(1)}, s32[10]{0:T(128)}, u32[]{:S(2)}) copy-start(s32[10]{0:T(128)} %stack.81.place_ref) | copy-start | bytes 124
  172.6 6.6 %copy-start.1 = (bf16[4,4,64,512]{3,2,1,0:T(8,128)(2,1)S(1)}, bf16[4,4,64,512]{3,2,1,0:T(8,128)(2,1)}, u32[]{:S(2)}) copy-start(bf16[4,4,64,512]{3,2,1,0:T(8,128)(2,1)} %get-tuple-element.295.refs_0_) | copy-start | bytes 3145732
  172.7 6.5 %collective-permute-start.22 = (bf16[4,4,64,512]{3,2,1,0:T(8,128)(2,1)}, bf16[4,4,64,512]{3,2,1,0:T(8,128)(2,1)S(1)}, u32[]{:S(2)}, u32[]{:S(2)}) collective-permute-start(bf16[4,4,64,512]{3,2,1,0:T(8,128)(2,1)} %get-tuple-element.296), channel_id=1, source_target_pairs={{0,1},{1,0},{2,3},{3,2},{4,5},{5,4},{6,7},{7,6},{8,9},{9,8},{10,11... | collective-permute-start | bytes 3145736 | tf_op jit(solution)/shard_map/ppermute | solution.py:933
  172.8 3.7 %collective-permute-start.23 = (bf16[512,512]{1,0:T(8,128)(2,1)}, bf16[512,512]{1,0:T(8,128)(2,1)S(1)}, u32[]{:S(2)}, u32[]{:S(2)}) collective-permute-start(bf16[512,512]{1,0:T(8,128)(2,1)} %get-tuple-element.305), channel_id=1, source_target_pairs={{0,1},{1,0},{2,3},{3,2},{4,5},{5,4},{6,7},{7,6},{8,9},{9,8},{10,11... | collective-permute-start | bytes 1572872 | tf_op jit(solution)/shard_map/ppermute | solution.py:933
  180.0 9.2 %collective-permute-start.24 = (bf16[256,512]{1,0:T(8,128)(2,1)S(1)}, bf16[256,512]{1,0:T(8,128)(2,1)S(1)}, u32[]{:S(2)}, u32[]{:S(2)}) collective-permute-start(bf16[256,512]{1,0:T(8,128)(2,1)S(1)} %get-tuple-element.310), channel_id=1, source_target_pairs={{0,8},{8,0},{16,24},{24,16},{1,9},{9,1},{17,25},{25,17},{2,10},{10... | collective-permute-start | bytes 786440 | tf_op jit(solution)/shard_map/ppermute | solution.py:952
  182.0 14.3 %collective-permute-start.25 = (bf16[256,512]{1,0:T(8,128)(2,1)S(1)}, bf16[256,512]{1,0:T(8,128)(2,1)S(1)}, u32[]{:S(2)}, u32[]{:S(2)}) collective-permute-start(bf16[256,512]{1,0:T(8,128)(2,1)S(1)} %get-tuple-element.311), channel_id=1, source_target_pairs={{0,16},{8,24},{16,0},{24,8},{1,17},{9,25},{17,1},{25,9},{2,18},{10... | collective-permute-start | bytes 786440 | tf_op jit(solution)/shard_map/ppermute | solution.py:952
  182.3 14.0 %collective-permute-start.26 = (bf16[256,512]{1,0:T(8,128)(2,1)S(1)}, bf16[256,512]{1,0:T(8,128)(2,1)S(1)}, u32[]{:S(2)}, u32[]{:S(2)}) collective-permute-start(bf16[256,512]{1,0:T(8,128)(2,1)S(1)} %get-tuple-element.312), channel_id=1, source_target_pairs={{0,24},{8,16},{16,8},{24,0},{1,25},{9,17},{17,9},{25,1},{2,26},{10... | collective-permute-start | bytes 786440 | tf_op jit(solution)/shard_map/ppermute | solution.py:952
  184.4 34.4 %copy-start.15 = (bf16[2,256,512]{2,1,0:T(8,128)(2,1)S(1)}, bf16[2,256,512]{2,1,0:T(8,128)(2,1)}, u32[]{:S(2)}) copy-start(bf16[2,256,512]{2,1,0:T(8,128)(2,1)} %copy-done.14) | copy-start | bytes 1572868
  184.4 34.4 %copy-start.17 = (bf16[2,256,512]{2,1,0:T(8,128)(2,1)S(1)}, bf16[2,256,512]{2,1,0:T(8,128)(2,1)}, u32[]{:S(2)}) copy-start(bf16[2,256,512]{2,1,0:T(8,128)(2,1)} %copy-done.16) | copy-start | bytes 1572868
  184.4 35.5 %collective-permute-start.33 = (bf16[2,256,512]{2,1,0:T(8,128)(2,1)S(1)}, bf16[2,256,512]{2,1,0:T(8,128)(2,1)S(1)}, u32[]{:S(2)}, u32[]{:S(2)}) collective-permute-start(bf16[2,256,512]{2,1,0:T(8,128)(2,1)S(1)} %get-tuple-element.334), channel_id=1, source_target_pairs={{0,0},{1,8},{2,2},{3,10},{4,4},{5,12},{6,6},{7,14},{8,1},{9,9},{10... | collective-permute-start | bytes 1572872 | tf_op jit(solution)/shard_map/ppermute | solution.py:924
  185.2 34.7 %collective-permute-start.34 = (bf16[2,256,512]{2,1,0:T(8,128)(2,1)S(1)}, bf16[2,256,512]{2,1,0:T(8,128)(2,1)}, u32[]{:S(2)}, u32[]{:S(2)}) collective-permute-start(bf16[2,256,512]{2,1,0:T(8,128)(2,1)S(1)} %get-tuple-element.335), channel_id=1, source_target_pairs={{0,24},{1,16},{2,26},{3,18},{4,28},{5,20},{6,30},{7,22},{8,25},{9,... | collective-permute-start | bytes 1572872 | tf_op jit(solution)/shard_map/ppermute | solution.py:924
  197.0 11.1 %collective-permute-start.27 = (bf16[192,512]{1,0:T(8,128)(2,1)S(1)}, bf16[192,512]{1,0:T(8,128)(2,1)}, u32[]{:S(2)}, u32[]{:S(2)}) collective-permute-start(bf16[192,512]{1,0:T(8,128)(2,1)S(1)} %get-tuple-element.326), channel_id=1, source_target_pairs={{0,2},{1,3},{2,0},{3,1},{4,6},{5,7},{6,4},{7,5},{8,10},{9,11},{10,... | collective-permute-start | bytes 589832 | tf_op jit(solution)/shard_map/ppermute | solution.py:960
  198.3 17.3 %collective-permute-start.28 = (bf16[192,512]{1,0:T(8,128)(2,1)S(1)}, bf16[192,512]{1,0:T(8,128)(2,1)}, u32[]{:S(2)}, u32[]{:S(2)}) collective-permute-start(bf16[192,512]{1,0:T(8,128)(2,1)S(1)} %get-tuple-element.327), channel_id=1, source_target_pairs={{0,4},{1,5},{2,6},{3,7},{4,0},{5,1},{6,2},{7,3},{8,12},{9,13},{10,... | collective-permute-start | bytes 589832 | tf_op jit(solution)/shard_map/ppermute | solution.py:960
  201.0 15.6 %collective-permute-start.29 = (bf16[192,512]{1,0:T(8,128)(2,1)S(1)}, bf16[192,512]{1,0:T(8,128)(2,1)}, u32[]{:S(2)}, u32[]{:S(2)}) collective-permute-start(bf16[192,512]{1,0:T(8,128)(2,1)S(1)} %get-tuple-element.328), channel_id=1, source_target_pairs={{0,6},{1,7},{2,4},{3,5},{4,2},{5,3},{6,0},{7,1},{8,14},{9,15},{10,... | collective-permute-start | bytes 589832 | tf_op jit(solution)/shard_map/ppermute | solution.py:960
  208.1 11.8 %collective-permute-start.30 = (bf16[272,512]{1,0:T(8,128)(2,1)S(1)}, bf16[272,512]{1,0:T(8,128)(2,1)S(1)}, u32[]{:S(2)}, u32[]{:S(2)}) collective-permute-start(bf16[272,512]{1,0:T(8,128)(2,1)S(1)} %get-tuple-element.331), channel_id=1, source_target_pairs={{0,8},{8,0},{16,24},{24,16},{1,9},{9,1},{17,25},{25,17},{2,10},{10... | collective-permute-start | bytes 835592 | tf_op jit(solution)/shard_map/ppermute | solution.py:952
  215.5 15.2 %collective-permute-start.31 = (bf16[272,512]{1,0:T(8,128)(2,1)S(1)}, bf16[272,512]{1,0:T(8,128)(2,1)S(1)}, u32[]{:S(2)}, u32[]{:S(2)}) collective-permute-start(bf16[272,512]{1,0:T(8,128)(2,1)S(1)} %get-tuple-element.332), channel_id=1, source_target_pairs={{0,16},{8,24},{16,0},{24,8},{1,17},{9,25},{17,1},{25,9},{2,18},{10... | collective-permute-start | bytes 835592 | tf_op jit(solution)/shard_map/ppermute | solution.py:952
  216.6 14.2 %collective-permute-start.32 = (bf16[272,512]{1,0:T(8,128)(2,1)S(1)}, bf16[272,512]{1,0:T(8,128)(2,1)S(1)}, u32[]{:S(2)}, u32[]{:S(2)}) collective-permute-start(bf16[272,512]{1,0:T(8,128)(2,1)S(1)} %get-tuple-element.333), channel_id=1, source_target_pairs={{0,24},{8,16},{16,8},{24,0},{1,25},{9,17},{17,9},{25,1},{2,26},{10... | collective-permute-start | bytes 835592 | tf_op jit(solution)/shard_map/ppermute | solution.py:952
  232.1 8.4 %collective-permute-start.37 = (bf16[336,512]{1,0:T(8,128)(2,1)S(1)}, bf16[336,512]{1,0:T(8,128)(2,1)S(1)}, u32[]{:S(2)}, u32[]{:S(2)}) collective-permute-start(bf16[336,512]{1,0:T(8,128)(2,1)S(1)} %pad_maximum_fusion.2.refs_0_), channel_id=1, source_target_pairs={{0,24},{8,16},{16,8},{24,0},{1,25},{9,17},{17,9},{25,1},{2,26},{10... | collective-permute-start | bytes 1032200 | tf_op jit(solution)/shard_map/ppermute | solution.py:952
  235.2 8.9 %collective-permute-start.36 = (bf16[336,512]{1,0:T(8,128)(2,1)S(1)}, bf16[336,512]{1,0:T(8,128)(2,1)S(1)}, u32[]{:S(2)}, u32[]{:S(2)}) collective-permute-start(bf16[336,512]{1,0:T(8,128)(2,1)S(1)} %pad_maximum_fusion.2.refs_0_), channel_id=1, source_target_pairs={{0,16},{8,24},{16,0},{24,8},{1,17},{9,25},{17,1},{25,9},{2,18},{10... | collective-permute-start | bytes 1032200 | tf_op jit(solution)/shard_map/ppermute | solution.py:952
  235.4 8.7 %collective-permute-start.35 = (bf16[336,512]{1,0:T(8,128)(2,1)S(1)}, bf16[336,512]{1,0:T(8,128)(2,1)S(1)}, u32[]{:S(2)}, u32[]{:S(2)}) collective-permute-start(bf16[336,512]{1,0:T(8,128)(2,1)S(1)} %pad_maximum_fusion.2.refs_0_), channel_id=1, source_target_pairs={{0,8},{8,0},{16,24},{24,16},{1,9},{9,1},{17,25},{25,17},{2,10},{10... | collective-permute-start | bytes 1032200 | tf_op jit(solution)/shard_map/ppermute | solution.py:952
  (23 other events, 43.4 us)
Sparse Core Ops, SparseCore 0:
  84.3 50.7 reduce-scatter.2
  146.8 56.5 reduce-scatter.4
